TPU v7x, 256 devices: a whole 4x4x8 slice. The times are simulated.
256 devices in a mesh: row: 16 (over y, x), col: 16 (over z, core).
Axes of the slice: x: 4, y: 4, z: 8, core: 2. Of those that a mesh axis runs over, the one named last changes fastest.
Arguments:
- inputs: bfloat16 [768, 8192], P('col', 'row'), may hold values from -6 to 6
- w_gate: bfloat16 [8192, 28672], P('row', 'col'), may hold values from -0.0625 to 0.0625
- w_up: bfloat16 [8192, 28672], P('row', 'col'), may hold values from -0.0625 to 0.0625
- w_down: bfloat16 [28672, 8192], P('col', 'row'), may hold values from -0.03125 to 0.03125
- cotangent: bfloat16 [768, 8192], P('col', 'row'), may hold values from -6 to 6
Outputs:
- output: bfloat16 [768, 8192], P('col', 'row')
- input_grad: bfloat16 [768, 8192], P('col', 'row')
- gate_grad: bfloat16 [8192, 28672], P('row', 'col')
- up_grad: bfloat16 [8192, 28672], P('row', 'col')
- down_grad: bfloat16 [28672, 8192], P('col', 'row')
All inputs are finite; a program needn't handle non-finite values.
Results may differ from a plain program's by a relative error of at most 0.035.
Values may be sent and summed in bfloat16 or wider, within the bound.
A program may use at most 128 MiB of HBM per device.

v0:
```python
import jax
import jax.numpy as jnp
from jax import lax
from jax.sharding import PartitionSpec as P

contract_rows = (((0,), (0,)), ((), ()))
contract_cols = (((1,), (1,)), ((), ()))


def local(inputs, w_gate, w_up, w_down, cotangent):
    inputs_all = lax.all_gather(inputs, "col", axis=0, tiled=True)
    hidden_width = w_gate.shape[1]
    row_block = inputs_all
    joined = lax.psum_scatter(
        jnp.concatenate(
            [
                jnp.dot(row_block, w_gate, preferred_element_type=jnp.float32),
                jnp.dot(row_block, w_up, preferred_element_type=jnp.float32),
            ],
            1,
        ).astype(jnp.bfloat16),
        "row",
        scatter_dimension=0,
        tiled=True,
    ).astype(jnp.float32)
    gate_own = joined[:, :hidden_width]
    up_own = joined[:, hidden_width:]
    hidden_own = (gate_own * jax.nn.sigmoid(gate_own) * up_own).astype(jnp.bfloat16)
    hidden_all = lax.all_gather(hidden_own, "row", axis=0, tiled=True)
    row_block = hidden_all
    output = lax.psum_scatter(
        jnp.dot(row_block, w_down, preferred_element_type=jnp.float32).astype(jnp.bfloat16),
        "col",
        scatter_dimension=0,
        tiled=True,
    )
    cotangent_all = lax.all_gather(cotangent, "col", axis=0, tiled=True)
    down_grad = lax.dot_general(
        hidden_all, cotangent_all, contract_rows, preferred_element_type=jnp.float32
    ).astype(jnp.bfloat16)
    row_block = cotangent_all
    hidden_grad = lax.psum_scatter(
        lax.dot_general(
            row_block, w_down, contract_cols, preferred_element_type=jnp.float32
        ).astype(jnp.bfloat16),
        "row",
        scatter_dimension=0,
        tiled=True,
    ).astype(jnp.float32)
    sigmoid_gate = jax.nn.sigmoid(gate_own)
    gate_delta = (
        hidden_grad * up_own * sigmoid_gate * (1.0 + gate_own * (1.0 - sigmoid_gate))
    ).astype(jnp.bfloat16)
    up_delta = (hidden_grad * gate_own * sigmoid_gate).astype(jnp.bfloat16)
    gate_delta_all, up_delta_all = (
        lax.all_gather(gate_delta, "row", axis=0, tiled=True),
        lax.all_gather(up_delta, "row", axis=0, tiled=True),
    )
    gate_grad = lax.dot_general(
        inputs_all, gate_delta_all, contract_rows, preferred_element_type=jnp.float32
    ).astype(jnp.bfloat16)
    up_grad = lax.dot_general(
        inputs_all, up_delta_all, contract_rows, preferred_element_type=jnp.float32
    ).astype(jnp.bfloat16)
    first_term = lax.dot_general(
        gate_delta_all, w_gate, contract_cols, preferred_element_type=jnp.float32
    )
    input_grad = lax.psum_scatter(
        (
            first_term
            + lax.dot_general(up_delta_all, w_up, contract_cols, preferred_element_type=jnp.float32)
        ).astype(jnp.bfloat16),
        "col",
        scatter_dimension=0,
        tiled=True,
    )
    return (output, input_grad, gate_grad, up_grad, down_grad)


def solution(mesh):
    return jax.shard_map(
        local,
        mesh=mesh,
        in_specs=(
            P("col", "row"),
            P("row", "col"),
            P("row", "col"),
            P("col", "row"),
            P("col", "row"),
        ),
        out_specs=(
            P("col", "row"),
            P("col", "row"),
            P("row", "col"),
            P("row", "col"),
            P("col", "row"),
        ),
        check_vma=False,
    )
```

profile of v0, /device:TPU:1, one launch (start us, length us, event | category | flops | bytes accessed | tf_op | source)
XLA Modules:
  0.0 488.2 jit_solution(6277281098951693596)
XLA Ops:
  7.2 23.9 %all_gather.15 = bf16[768,512]{1,0:T(8,128)(2,1)S(1)} all-gather(bf16[48,512]{1,0:T(8,128)(2,1)} %param.5), channel_id=1, replica_groups=mesh['row'=16,'col'=16] {'col'}, dimensions={0}, use_global_device_ids=true | all-gather | bytes 835584 | tf_op jit(solution)/shard_map/all_gather | solution.py:11
  31.1 3.1 convolution_convert_fusion.1
  34.2 1.6 convolution_convert_fusion.2
  35.8 2.8 pad_maximum_fusion
  39.4 16.6 %all_gather.17 = bf16[768,512]{1,0:T(8,128)(2,1)S(1)} all-gather(bf16[48,512]{1,0:T(8,128)(2,1)S(1)} %copy-done.3), channel_id=1, replica_groups=mesh['row'=16,'col'=16] {'col'}, dimensions={0}, use_global_device_ids=true | all-gather | bytes 835584 | tf_op jit(solution)/shard_map/all_gather | solution.py:37
  56.0 0.9 copy-done.1
  57.0 4.7 convolution_convert_fusion
  61.7 58.4 %reduce-scatter.5.cloned.1.call-done = bf16[48,3584]{1,0:T(8,128)(2,1)} async-done(((bf16[768,3584]{1,0:T(8,128)(2,1)}), bf16[48,3584]{1,0:T(8,128)(2,1)}) %reduce-scatter.5.cloned.1.call-update) | async-done | bytes 344080 | tf_op jit(solution)/shard_map/reduce_scatter | solution.py:14
  120.2 1.0 convert_element_type.40
  121.2 81.8 %reduce-scatter.9.cloned.1.call-done = bf16[48,1792]{1,0:T(8,128)(2,1)} async-done(((bf16[768,1792]{1,0:T(8,128)(2,1)}), bf16[48,1792]{1,0:T(8,128)(2,1)}) %reduce-scatter.9.cloned.1.call-update) | async-done | bytes 172048 | tf_op jit(solution)/shard_map/reduce_scatter | solution.py:42
  203.0 1.9 fusion.6
  206.1 52.3 %all-gather.6.cloned.1.call-done = bf16[768,1792]{1,0:T(8,128)(2,1)} async-done(((bf16[48,1792]{1,0:T(8,128)(2,1)}), bf16[768,1792]{1,0:T(8,128)(2,1)}) %all-gather.6.cloned.1.call-update) | async-done | bytes 2752528 | tf_op jit(solution)/shard_map/all_gather | solution.py:56
  258.4 4.5 fusion.7
  262.9 49.3 %all-gather.8.cloned.1.call-done = bf16[768,1792]{1,0:T(8,128)(2,1)} async-done(((bf16[48,1792]{1,0:T(8,128)(2,1)}), bf16[768,1792]{1,0:T(8,128)(2,1)}) %all-gather.8.cloned.1.call-update) | async-done | bytes 2752528 | tf_op jit(solution)/shard_map/all_gather | solution.py:57
  312.2 5.3 %add_convert_fusion = bf16[768,512]{1,0:T(8,128)(2,1)} fusion(f32[768,512]{1,0:T(8,128)} %fusion.7, bf16[768,1792]{1,0:T(8,128)(2,1)} %all-gather.8.cloned.1.call-done, bf16[512,1792]{1,0:T(8,128)(2,1)} %param.7), kind=kOutput, calls=%fused_computation.9 | convolution fusion | flops 1410072576 | bytes 6946816 | tf_op jit(solution)/shard_map/dot_general | solution.py:71
  317.8 48.3 %all-gather.4.cloned.1.call-done = bf16[768,1792]{1,0:T(8,128)(2,1)} async-done(((bf16[48,1792]{1,0:T(8,128)(2,1)}), bf16[768,1792]{1,0:T(8,128)(2,1)}) %all-gather.4.cloned.1.call-update) | async-done | bytes 2752528 | tf_op jit(solution)/shard_map/all_gather | solution.py:29
  366.1 4.8 convolution_convert_fusion.6
  370.9 4.6 fusion
  375.5 3.8 copy.10
  379.3 4.7 fusion.1
  384.0 3.9 copy.11
  387.9 4.6 convolution_convert_fusion.3
  392.5 30.1 %reduce-scatter.11.cloned.1.call-done = bf16[48,512]{1,0:T(8,128)(2,1)} async-done(((bf16[768,512]{1,0:T(8,128)(2,1)}), bf16[48,512]{1,0:T(8,128)(2,1)}) %reduce-scatter.11.cloned.1.call-update) | async-done | bytes 49168 | tf_op jit(solution)/shard_map/reduce_scatter | solution.py:68
  422.6 58.8 %reduce-scatter.7.cloned.1.call-done = bf16[48,512]{1,0:T(8,128)(2,1)} async-done(((bf16[768,512]{1,0:T(8,128)(2,1)}), bf16[48,512]{1,0:T(8,128)(2,1)}) %reduce-scatter.7.cloned.1.call-update) | async-done | bytes 49168 | tf_op jit(solution)/shard_map/reduce_scatter | solution.py:31
  (21 shorter events, 2.3 us)
Async XLA Ops:
  7.2 27.0 %copy-start = (bf16[512,1792]{1,0:T(8,128)(2,1)S(1)}, bf16[512,1792]{1,0:T(8,128)(2,1)}, u32[]{:S(2)}) copy-start(bf16[512,1792]{1,0:T(8,128)(2,1)} %param.6) | copy-start | bytes 5505028
  7.2 113.0 %reduce-scatter.5.cloned.1.call-start = ((), (), s32[]{:S(2)}) async-start(), calls=%async_computation.4 | async-start | bytes 5849088 | tf_op jit(solution)/shard_map/reduce_scatter | solution.py:14
  38.6 0.8 copy-start.3
  38.6 164.3 %reduce-scatter.9.cloned.1.call-start = ((), (), s32[]{:S(2)}) async-start(), calls=%async_computation.7 | async-start | bytes 2924544 | tf_op jit(solution)/shard_map/reduce_scatter | solution.py:42
  56.0 0.9 copy-start.1
  61.7 196.7 %all-gather.6.cloned.1.call-start = ((), (), s32[]{:S(2)}) async-start(), calls=%async_computation.8 | async-start | bytes 2924544 | tf_op jit(solution)/shard_map/all_gather | solution.py:56
  204.9 107.4 %all-gather.8.cloned.1.call-start = ((), (), s32[]{:S(2)}) async-start(), calls=%async_computation.9 | async-start | bytes 2924544 | tf_op jit(solution)/shard_map/all_gather | solution.py:57
  205.4 160.6 %all-gather.4.cloned.1.call-start = ((), (), s32[]{:S(2)}) async-start(), calls=%async_computation.5 | async-start | bytes 2924544 | tf_op jit(solution)/shard_map/all_gather | solution.py:29
  206.0 216.6 %reduce-scatter.11.cloned.1.call-start = ((), (), s32[]{:S(2)}) async-start(), calls=%async_computation.10 | async-start | bytes 835584 | tf_op jit(solution)/shard_map/reduce_scatter | solution.py:68
  317.6 163.8 %reduce-scatter.7.cloned.1.call-start = ((), (), s32[]{:S(2)}) async-start(), calls=%async_computation.6 | async-start | bytes 835584 | tf_op jit(solution)/shard_map/reduce_scatter | solution.py:31
  384.0 3.9 copy-start.2
Sparse Core Ops, SparseCore 0:
  38.8 81.3 reduce-scatter.4
  123.8 79.1 reduce-scatter.8
  206.0 52.3 all-gather.5
  261.2 50.9 all-gather.7
  315.1 50.9 all-gather.3
  369.0 53.5 reduce-scatter.10
  425.9 55.4 reduce-scatter.6
where the time goes:
time: 491 us; the launch traced here: 488 us
  waiting for transfers between devices  380 us (77%)
  blocking collectives  40.5 us (8%)
  matrix products  37.9 us (8%)
  between operations  14.2 us (3%)
  local copies, waits for them, and re-layouts  9.35 us (2%)
  other arithmetic  5.71 us (1%)
    reduce_scatter x1, waiting for transfers between devices, local(): lax.psum_scatter(lax.dot_general(row_block, w_down, contract_cols, prefer...  81.8 us
    reduce_scatter x1, waiting for transfers between devices, local(): lax.psum_scatter(jnp.dot(row_block, w_down, preferred_element_type=jnp.fl...  58.8 us
    reduce_scatter x1, waiting for transfers between devices, local(): lax.psum_scatter(jnp.concatenate([jnp.dot(row_block, w_gate, preferred_el...  58.4 us
    all_gather x1, waiting for transfers between devices, local(): lax.all_gather(gate_delta, 'row', axis=0, tiled=True)  52.3 us
    all_gather x1, waiting for transfers between devices, local(): lax.all_gather(up_delta, 'row', axis=0, tiled=True)  49.3 us
    all_gather x1, waiting for transfers between devices, local(): hidden_all = lax.all_gather(hidden_own, 'row', axis=0, tiled=True)  48.3 us
    reduce_scatter x1, waiting for transfers between devices, local(): lax.psum_scatter((first_term + lax.dot_general(up_delta_all, w_up, contra...  30.1 us
    all_gather x1, blocking collectives, local(): inputs_all = lax.all_gather(inputs, 'col', axis=0, tiled=True)  23.9 us
  transfers between devices with their start and end apart: 7, of which 7 were waited for; matrix products, arithmetic and copies ran while one was open for 9% of the time, Pallas kernels for 0%

commit v1 on v0

v1 whole, which is shorter than its diff:
```python
import functools

import jax
import jax.numpy as jnp
from jax import lax
from jax.experimental import pallas as pl
from jax.experimental.pallas import tpu as pltpu
from jax.sharding import PartitionSpec as P

MESH = pl.DeviceIdType.MESH
ROWS = 16
CHUNKS = 3
BLOCKS = 16
CHIPS = 8
SETS = ((0, 512), (512, 512), (1024, 384), (1408, 384))
D, F = 512, 1792
WIDE = 896
BASE = (0, 8, 12, 14)

contract_rows = (((0,), (0,)), ((), ()))
contract_cols = (((1,), (1,)), ((), ()))


def place(stream, block):
    bits = [(block >> (3 - d)) & 1 for d in range(4)]
    index = 0
    for step in range(4):
        index = index * 2 + bits[(stream + step) % 4]
    return index


PLACES = [[place(j, k) for k in range(BLOCKS)] for j in range(4)]


def kernel(
    x_hbm, wg_hbm, wu_hbm, wd_hbm, ct_hbm,
    out_hbm, ig_hbm, gg_hbm, ug_hbm, dg_hbm,
    x_in, ct_in, xs, cts, wg, wu, wd,
    p_gu, r_gu, d_all, acc_g, acc_u, acc_d, gg, ug, dg, o_part, o_sib, o_z, o_fin,
    p_h0, p_h1, p_h2, p_h3, r_h0, r_h1, r_h2, r_h3, h0, h1, h2, h3,
    load_sem, store_sem, ssem, rsem, zs_sem, zr_sem,
):
    p_hg, r_hg, h_all = (p_h0, p_h1, p_h2, p_h3), (r_h0, r_h1, r_h2, r_h3), (h0, h1, h2, h3)
    row, col = lax.axis_index("row"), lax.axis_index("col")
    y, x = row // 4, row % 4
    z, core = col // 2, col % 2
    partner = (
        (y * 4 + x + 1 - 2 * (x % 2), col),
        ((y + 1 - 2 * (y % 2)) * 4 + x, col),
        (y * 4 + 3 - x, col),
        ((3 - y) * 4 + x, col),
    )
    bits = (((x + 1) // 2) % 2, ((y + 1) // 2) % 2, x // 2, y // 2)
    mine = []
    for j in range(4):
        index = 0
        for step in range(4):
            index = index * 2 + bits[(j + step) % 4]
        mine.append(index)
    sibling = (row, z * 2 + 1 - core)
    along = [(row, lax.rem(z + d, CHIPS) * 2 + core) for d in range(1, CHIPS)]

    loads = []
    for i, (src, dst) in enumerate(
        ((x_hbm, x_in), (ct_hbm, ct_in), (wg_hbm, wg), (wu_hbm, wu), (wd_hbm, wd))
    ):
        loads.append(pltpu.make_async_copy(src, dst, load_sem.at[i]))
        loads[-1].start()

    barrier = pltpu.get_barrier_semaphore()
    peers = list(partner) + along + [sibling]
    for peer in peers:
        pl.semaphore_signal(barrier, inc=1, device_id=peer, device_id_type=MESH)
    loads[0].wait()
    loads[1].wait()
    pl.semaphore_wait(barrier, len(peers))

    sent = []

    def send(src, dst, send_sem, recv_sem, device):
        copy = pltpu.make_async_remote_copy(
            src_ref=src, dst_ref=dst, send_sem=send_sem, recv_sem=recv_sem,
            device_id=device, device_id_type=MESH,
        )
        copy.start()
        sent.append(copy)
        return copy

    def gather_start(kind, c):
        buffer, own = ((xs, x_in), (cts, ct_in))[kind]
        block = own[c * ROWS:(c + 1) * ROWS, :]
        buffer[c, core, z] = block
        return [
            send(buffer.at[c, core, z], buffer.at[c, core, z], zs_sem.at[kind, c, d], zr_sem.at[kind, c, d], along[d])
            for d in range(CHIPS - 1)
        ]

    def gather_share(kind, c, copies):
        buffer = (xs, cts)[kind]
        for copy in copies:
            copy.wait_recv()
        return send(buffer.at[c, core], buffer.at[c, core], zs_sem.at[kind, c, 7], zr_sem.at[kind, c, 7], sibling)

    def rows_of(buffer, c):
        return buffer[c].reshape(BLOCKS * ROWS, D)

    def summed(lane, c, j):
        return (p_gu.at[c, j], r_gu.at[c, j]) if lane == 0 else (p_hg[j].at[c], r_hg[j].at[c])

    def gathered(lane, c, j):
        return h_all[j].at[c] if lane == 0 else d_all.at[c, j]

    flight = {}

    def reduce_send(lane, c, j, step):
        part, arrive = summed(lane, c, j)
        half = 8 >> step
        own = mine[j] // half * half
        other = own + half - 2 * half * (mine[j] // half % 2)
        flight[lane, c, j, step] = send(
            part.at[pl.ds(other, half)], arrive.at[pl.ds(BASE[step], half)],
            ssem.at[lane, c, j, step], rsem.at[lane, c, j, step], partner[(j + step) % 4],
        )

    def reduce_add(lane, c, j, step, first, count):
        part, arrive = summed(lane, c, j)
        half = 8 >> step
        own = mine[j] // half * half

        def body(i, carry):
            at = first + i
            part[at] = (
                part[at].astype(jnp.float32) + arrive[BASE[step] + at - own].astype(jnp.float32)
            ).astype(jnp.bfloat16)
            return carry

        lax.fori_loop(0, count, body, 0)

    def reduce_step(lane, c, j, step):
        flight[lane, c, j, step - 1].wait_recv()
        half = 8 >> step
        own = mine[j] // half * half
        other = own + half - 2 * half * (mine[j] // half % 2)
        reduce_add(lane, c, j, step - 1, other, half)
        reduce_send(lane, c, j, step)
        reduce_add(lane, c, j, step - 1, own, half)

    def reduce_last(lane, c, j):
        flight[lane, c, j, 3].wait_recv()
        part, arrive = summed(lane, c, j)
        return part[mine[j]].astype(jnp.float32) + arrive[BASE[3]].astype(jnp.float32)

    def gather_send(lane, c, j, step):
        buffer = gathered(lane, c, j)
        if step > 0:
            flight[lane, c, j, 3 + step].wait_recv()
        size = 1 << step
        region = buffer.at[pl.ds(mine[j] // size * size, size)]
        flight[lane, c, j, 4 + step] = send(
            region, region, ssem.at[lane, c, j, 4 + step], rsem.at[lane, c, j, 4 + step], partner[(j + 3 - step) % 4]
        )

    def store_partial(ref, j, lo, value):
        width = value.shape[1]
        value = value.astype(jnp.bfloat16)
        for k in range(BLOCKS):
            ref[PLACES[j][k], :, lo:lo + width] = value[k * ROWS:(k + 1) * ROWS, :]

    def gate_up(c, j):
        other = (j + 2) % 4
        value = rows_of(xs, c)
        lo, width = SETS[j]
        store_partial(p_gu.at[c, j], j, 0, jnp.dot(value, wg[:, lo:lo + width], preferred_element_type=jnp.float32))
        at = width
        lo, width = SETS[other]
        store_partial(p_gu.at[c, j], j, at, jnp.dot(value, wu[:, lo:lo + width], preferred_element_type=jnp.float32))

    def hidden_grad(c, j):
        lo, width = SETS[j]
        value = lax.dot_general(rows_of(cts, c), wd[lo:lo + width, :], contract_cols, preferred_element_type=jnp.float32)
        store_partial(p_hg[j].at[c], j, 0, value)

    kept = {}

    def make_hidden(c):
        sums = [reduce_last(0, c, j) for j in range(4)]
        for j in range(4):
            width = SETS[j][1]
            gate = sums[j][:, :width]
            up = sums[(j + 2) % 4][:, WIDE - width:]
            h_all[j][c, mine[j]] = (gate * jax.nn.sigmoid(gate) * up).astype(jnp.bfloat16)
            gather_send(0, c, j, 0)

    def make_deltas(c):
        sums = []
        for j in range(4):
            part, arrive = summed(0, c, j)
            sums.append(part[mine[j]].astype(jnp.float32) + arrive[BASE[3]].astype(jnp.float32))
        for j in range(4):
            other = (j + 2) % 4
            width = SETS[j][1]
            gate = sums[j][:, :width]
            up = sums[other][:, WIDE - width:]
            grad = reduce_last(1, c, j)
            s = jax.nn.sigmoid(gate)
            d_all[c, j, mine[j], :, :width] = (grad * up * s * (1.0 + gate * (1.0 - s))).astype(jnp.bfloat16)
            d_all[c, other, mine[other], :, WIDE - width:] = (grad * gate * s).astype(jnp.bfloat16)
        for j in range(4):
            gather_send(1, c, j, 0)

    def tokens(ref, c, j, lo, width):
        return jnp.concatenate([ref[c, PLACES[j][k], :, lo:lo + width] for k in range(BLOCKS)], axis=0)

    def hidden_of(c, j):
        return tokens(h_all[j], c, j, 0, SETS[j][1])

    def gate_delta_of(c, j):
        return tokens(d_all.at[:, j], c, j, 0, SETS[j][1])

    def up_delta_of(c, j):
        other = (j + 2) % 4
        return tokens(d_all.at[:, other], c, other, WIDE - SETS[j][1], SETS[j][1])

    def wait_gathered(lane, c):
        for j in range(4):
            flight[lane, c, j, 7].wait_recv()

    def scatter_start(kind, c, total):
        o_part[kind, c] = total.astype(jnp.bfloat16).reshape(2, CHIPS, ROWS, D)
        return send(o_part.at[kind, c, 1 - core], o_sib.at[kind, c], zs_sem.at[2 + kind, c, 7], zr_sem.at[2 + kind, c, 7], sibling)

    def scatter_along(kind, c, copy):
        copy.wait_recv()

        def body(i, carry):
            o_part[kind, c, core, i] = (
                o_part[kind, c, core, i].astype(jnp.float32) + o_sib[kind, c, i].astype(jnp.float32)
            ).astype(jnp.bfloat16)
            return carry

        lax.fori_loop(0, CHIPS, body, 0)
        return [
            send(
                o_part.at[kind, c, core, lax.rem(z + d + 1, CHIPS)], o_z.at[kind, c, d],
                zs_sem.at[2 + kind, c, d], zr_sem.at[2 + kind, c, d], along[d],
            )
            for d in range(CHIPS - 1)
        ]

    def scatter_end(kind, c, copies):
        for copy in copies:
            copy.wait_recv()
        total = o_part[kind, c, core, z].astype(jnp.float32)
        for d in range(CHIPS - 1):
            total = total + o_z[kind, c, d].astype(jnp.float32)
        o_fin[kind, c * ROWS:(c + 1) * ROWS, :] = total.astype(jnp.bfloat16)

    def output_part(c):
        total = None
        for j in range(4):
            lo, width = SETS[j]
            term = jnp.dot(hidden_of(c, j), wd[lo:lo + width, :], preferred_element_type=jnp.float32)
            total = term if total is None else total + term
        return scatter_start(0, c, total)

    def input_grad_part(c):
        total = None
        for j in range(4):
            lo, width = SETS[j]
            term = lax.dot_general(
                gate_delta_of(c, j), wg[:, lo:lo + width], contract_cols, preferred_element_type=jnp.float32
            ) + lax.dot_general(
                up_delta_of(c, j), wu[:, lo:lo + width], contract_cols, preferred_element_type=jnp.float32
            )
            total = term if total is None else total + term
        return scatter_start(1, c, total)

    def product(left, right, chunks):
        a = jnp.concatenate([left(c) for c in chunks], axis=0) if len(chunks) > 1 else left(chunks[0])
        b = jnp.concatenate([right(c) for c in chunks], axis=0) if len(chunks) > 1 else right(chunks[0])
        return lax.dot_general(a, b, contract_rows, preferred_element_type=jnp.float32)

    def down_grads(chunks, last):
        for j in range(4):
            lo, width = SETS[j]
            value = product(lambda c: hidden_of(c, j), lambda c: rows_of(cts, c), chunks)
            if last:
                dg[lo:lo + width, :] = (acc_d[lo:lo + width, :] + value).astype(jnp.bfloat16)
            else:
                acc_d[lo:lo + width, :] = value

    def input_side_grads(chunks, last):
        for j in range(4):
            lo, width = SETS[j]
            for acc, res, of in ((acc_g, gg, gate_delta_of), (acc_u, ug, up_delta_of)):
                value = product(lambda c: rows_of(xs, c), lambda c: of(c, j), chunks)
                if last:
                    res[:, lo:lo + width] = (acc[:, lo:lo + width] + value).astype(jnp.bfloat16)
                else:
                    acc[:, lo:lo + width] = value

    x_fly, ct_fly, share = {}, {}, {}
    x_fly[0] = gather_start(0, 0)
    ct_fly[0] = gather_start(1, 0)
    share[0, 0] = gather_share(0, 0, x_fly[0])
    loads[2].wait()
    loads[3].wait()
    share[0, 0].wait_recv()
    for j in range(4):
        gate_up(0, j)
        reduce_send(0, 0, j, 0)
    share[1, 0] = gather_share(1, 0, ct_fly[0])
    for c in (1, 2):
        x_fly[c] = gather_start(0, c)
        ct_fly[c] = gather_start(1, c)
    loads[4].wait()
    share[1, 0].wait_recv()
    for j in range(4):
        hidden_grad(0, j)
        reduce_send(1, 0, j, 0)

    def open_chunk(c):
        for j in range(4):
            reduce_send(0, c, j, 0)
        for j in range(4):
            reduce_send(1, c, j, 0)

    def prepare(c):
        share[0, c] = gather_share(0, c, x_fly[c])
        share[1, c] = gather_share(1, c, ct_fly[c])
        share[0, c].wait_recv()
        for j in range(4):
            gate_up(c, j)
        share[1, c].wait_recv()
        for j in range(4):
            hidden_grad(c, j)

    def advance(c, t):
        if t == 0:
            open_chunk(c)
        elif t < 4:
            for lane in (0, 1):
                for j in range(4):
                    reduce_step(lane, c, j, t)
        elif t == 4:
            make_hidden(c)
            make_deltas(c)
        else:
            for lane in (0, 1):
                for j in range(4):
                    gather_send(lane, c, j, t - 4)

    scatter = {}
    prepare(1)
    advance(0, 1)
    advance(0, 2)
    advance(1, 0)
    prepare(2)
    advance(0, 3)
    advance(1, 1)
    advance(0, 4)
    advance(1, 2)
    advance(2, 0)
    advance(0, 5)
    advance(1, 3)
    advance(2, 1)
    advance(1, 4)
    advance(2, 2)
    advance(0, 6)
    advance(2, 3)
    advance(1, 5)
    advance(0, 7)
    advance(2, 4)
    advance(1, 6)
    advance(2, 5)
    advance(1, 7)
    wait_gathered(0, 0)
    scatter[0, 0] = output_part(0)
    wait_gathered(1, 0)
    scatter[1, 0] = input_grad_part(0)
    advance(2, 6)
    wait_gathered(0, 1)
    scatter[0, 1] = output_part(1)
    wait_gathered(1, 1)
    scatter[1, 1] = input_grad_part(1)
    advance(2, 7)
    for c in (0, 1):
        for kind in (0, 1):
            scatter[kind, c] = scatter_along(kind, c, scatter[kind, c])
    down_grads((0, 1), False)
    input_side_grads((0, 1), False)
    wait_gathered(0, 2)
    scatter[0, 2] = output_part(2)
    down_grads((2,), True)
    stores = [pltpu.make_async_copy(dg, dg_hbm, store_sem.at[0])]
    stores[-1].start()
    scatter[0, 2] = scatter_along(0, 2, scatter[0, 2])
    for c in (0, 1):
        for kind in (0, 1):
            scatter_end(kind, c, scatter[kind, c])
    wait_gathered(1, 2)
    scatter[1, 2] = input_grad_part(2)
    scatter_end(0, 2, scatter[0, 2])
    scatter[1, 2] = scatter_along(1, 2, scatter[1, 2])
    input_side_grads((2,), True)
    for i, (src, dst) in enumerate(((gg, gg_hbm), (ug, ug_hbm), (o_fin.at[0], out_hbm))):
        stores.append(pltpu.make_async_copy(src, dst, store_sem.at[1 + i]))
        stores[-1].start()
    scatter_end(1, 2, scatter[1, 2])
    stores.append(pltpu.make_async_copy(o_fin.at[1], ig_hbm, store_sem.at[4]))
    stores[-1].start()
    for copy in sent:
        copy.wait_send()
    for copy in stores:
        copy.wait()


def local(inputs, w_gate, w_up, w_down, cotangent):
    bf16, f32 = jnp.bfloat16, jnp.float32
    vmem = pltpu.VMEM
    scratch = [
        vmem((CHUNKS * ROWS, D), bf16),
        vmem((CHUNKS * ROWS, D), bf16),
        vmem((CHUNKS, 2, CHIPS, ROWS, D), bf16),
        vmem((CHUNKS, 2, CHIPS, ROWS, D), bf16),
        vmem((D, F), bf16),
        vmem((D, F), bf16),
        vmem((F, D), bf16),
        vmem((CHUNKS, 4, BLOCKS, ROWS, WIDE), bf16),
        vmem((CHUNKS, 4, BLOCKS - 1, ROWS, WIDE), bf16),
        vmem((CHUNKS, 4, BLOCKS, ROWS, WIDE), bf16),
        vmem((D, F), f32),
        vmem((D, F), f32),
        vmem((F, D), f32),
        vmem((D, F), bf16),
        vmem((D, F), bf16),
        vmem((F, D), bf16),
        vmem((2, CHUNKS, 2, CHIPS, ROWS, D), bf16),
        vmem((2, CHUNKS, CHIPS, ROWS, D), bf16),
        vmem((2, CHUNKS, CHIPS - 1, ROWS, D), bf16),
        vmem((2, CHUNKS * ROWS, D), bf16),
    ]
    for count in (BLOCKS, BLOCKS - 1, BLOCKS):
        scratch += [vmem((CHUNKS, count, ROWS, width), bf16) for _, width in SETS]
    dma = pltpu.SemaphoreType.DMA
    scratch += [
        dma((5,)), dma((5,)),
        dma((2, CHUNKS, 4, 8)), dma((2, CHUNKS, 4, 8)),
        dma((4, CHUNKS, 8)), dma((4, CHUNKS, 8)),
    ]
    shape = jax.ShapeDtypeStruct
    return pl.pallas_call(
        kernel,
        out_shape=(
            shape(inputs.shape, bf16), shape(inputs.shape, bf16),
            shape(w_gate.shape, bf16), shape(w_up.shape, bf16), shape(w_down.shape, bf16),
        ),
        in_specs=[pl.BlockSpec(memory_space=pl.ANY)] * 5,
        out_specs=[pl.BlockSpec(memory_space=pl.ANY)] * 5,
        scratch_shapes=scratch,
        compiler_params=pltpu.CompilerParams(
            collective_id=0, has_side_effects=True, vmem_limit_bytes=62 * 2**20
        ),
    )(inputs, w_gate, w_up, w_down, cotangent)


def solution(mesh):
    return jax.shard_map(
        local,
        mesh=mesh,
        in_specs=(P("col", "row"), P("row", "col"), P("row", "col"), P("col", "row"), P("col", "row")),
        out_specs=(P("col", "row"), P("col", "row"), P("row", "col"), P("row", "col"), P("col", "row")),
        check_vma=False,
    )
```

time: 491 us -> 143 us (0.29)
  waiting for transfers between devices: 380 us -> 0 us
  Pallas kernels: 0 us -> 133 us
  blocking collectives: 40.5 us -> 0 us
  matrix products: 37.9 us -> 0 us
  between operations: 14.2 us -> 0.65 us
  other arithmetic: 5.71 us -> 0 us
    reduce_scatter x4 -> x0, waiting for transfers between devices: 229 us -> none  [the longest x1 81.8 us: local(): lax.psum_scatter(lax.dot_general(row_block, w_down, contract_cols, prefer...]
    all_gather x3 -> x0, waiting for transfers between devices: 150 us -> none  [the longest x1 52.3 us: local(): lax.all_gather(gate_delta, 'row', axis=0, tiled=True)]
    pallas_call x0 -> x1, Pallas kernels: none -> 133 us  [local(): pl.pallas_call(kernel, out_shape=(shape(inputs.shape, bf16), shape(inputs...]
    all_gather x2 -> x0, blocking collectives: 40.5 us -> none  [the longest x1 23.9 us: local(): inputs_all = lax.all_gather(inputs, 'col', axis=0, tiled=True)]
    dot_general x9 -> x0, matrix products: 37.9 us -> none  [the longest x1 5.31 us: local(): lax.dot_general(up_delta_all, w_up, contract_cols, preferred_element_type...]
  transfers between devices with their start and end apart: 7 -> 0, of which waited for: 7 -> 0; matrix products, arithmetic and copies ran while one was open for 9% -> 0% of each run, Pallas kernels for 0% -> 0%
where the time goes in v1:
time: 143 us
  Pallas kernels  133 us (93%)
  local copies, waits for them, and re-layouts  9.21 us (6%)
    pallas_call x1, Pallas kernels, local(): pl.pallas_call(kernel, out_shape=(shape(inputs.shape, bf16), shape(inputs...  133 us
    unnamed x9, local copies, waits for them, and re-layouts  9.21 us

profile of v1, /device:TPU:1, one launch (start us, length us, event | category | flops | bytes accessed | tf_op | source)
XLA Modules:
  0.0 143.1 jit_solution(9573335715185866509)
XLA Ops:
  0.6 133.3 %shard_map.92 = (bf16[48,512]{1,0:T(8,128)(2,1)}, bf16[48,512]{1,0:T(8,128)(2,1)}, bf16[512,1792]{1,0:T(8,128)(2,1)}, bf16[512,1792]{1,0:T(8,128)(2,1)}, bf16[1792,512]{1,0:T(8,128)(2,1)}) custom-call(bf16[48,512]{1,0:T(8,128)(2,1)} %x_hbm.1, bf16[512,1792]{1,0:T(8,128)(2,1)} %wg_hbm.1, bf16[512,1792]{1,0:T(8,128)(2,1)} %wu_hbm.1, bf16[1792,512]{1,0:T(8,128)(2,1)} %wd_hbm.1, ...), custom_call_target="tpu_custom_call" | custom-call | tf_op jit(solution)/shard_map/pallas_call | solution.py:452
  133.9 1.4 copy.15
  135.3 1.4 copy.16
  136.8 0.0 copy-start.1
  136.8 3.0 %copy.17 = bf16[512,1792]{1,0:T(8,128)(2,1)} copy(bf16[512,1792]{1,0:T(8,128)(2,1)} %get-tuple-element.12) | data formatting | bytes 3670016
  139.8 0.0 copy-done.1
  139.8 0.0 copy-start
  139.8 1.2 copy.18
  141.0 0.9 copy-done
  141.9 1.2 copy.19
Async XLA Ops:
  136.8 3.0 %copy-start.1 = (bf16[512,1792]{1,0:T(8,128)(2,1)S(1)}, bf16[512,1792]{1,0:T(8,128)(2,1)}, u32[]{:S(2)}) copy-start(bf16[512,1792]{1,0:T(8,128)(2,1)} %get-tuple-element.13) | copy-start | bytes 5505028
  139.8 2.2 %copy-start = (bf16[1792,512]{1,0:T(8,128)(2,1)S(1)}, bf16[1792,512]{1,0:T(8,128)(2,1)}, u32[]{:S(2)}) copy-start(bf16[1792,512]{1,0:T(8,128)(2,1)} %get-tuple-element.14) | copy-start | bytes 5505028

commit v2 on v0

v2 whole, which is shorter than its diff:
```python
import jax
import jax.numpy as jnp
from jax import lax
from jax.experimental import pallas as pl
from jax.experimental.pallas import tpu as pltpu
from jax.sharding import PartitionSpec as P

MESH = pl.DeviceIdType.MESH
ROWS = 16
OWN = 48
CHUNKS = 3
BLOCKS = 16
CHIPS = 8
SETS = ((0, 512), (512, 512), (1024, 384), (1408, 384))
D, F = 512, 1792
WIDE = 896
HALF = 128
PARTS = 4
BASE = (0, 8, 12, 14)

SPOT = {1: 0, -1: 48, 0: 96, 2: 144, -2: 192, 4: 240, 3: 288, -3: 336}
FIRST = (0, 256, 128)
GROUPS = ((1, -1), (4, 3, -3), (2, -2))
SPANS = ((0, 96), (240, 144), (144, 96))
PARCELS = (
    ((1, 0, 48, 0), (-1, 48, 48, 0)),
    ((4, 0, 32, 16), (3, 32, 48, 0), (-3, 80, 48, 0)),
    ((4, 112, 16, 0), (2, 16, 48, 0), (-2, 64, 48, 0)),
)
LANDED = ((0, 96), (256, 128), (144, 112))

contract_rows = (((0,), (0,)), ((), ()))
contract_cols = (((1,), (1,)), ((), ()))

ORDER = (
    ("x", 0), ("c", 0), ("sx", 0), ("x", 1), ("x", 2), ("sc", 0), ("c", 2), ("c", 1), ("gu", 0, 2), ("gu", 0, 3),
    ("gu", 0, 1), ("hg", 0, 3), ("hg", 0, 0), ("hg", 0, 2), ("hg", 0, 1), ("gu", 0, 0), ("r", 1, 0, 2, 1), ("sx",
    1), ("r", 0, 0, 2, 1), ("r", 0, 0, 3, 1), ("r", 0, 0, 1, 1), ("sx", 2), ("gu", 1, 3), ("gu", 1, 1), ("gu", 1,
    0), ("gu", 2, 3), ("r", 1, 0, 3, 1), ("r", 1, 0, 1, 1), ("sc", 2), ("gu", 2, 2), ("r", 1, 0, 0, 1), ("r", 0, 0,
    0, 1), ("r", 1, 0, 2, 2), ("gu", 2, 0), ("gu", 1, 2), ("gu", 2, 1), ("r", 0, 0, 2, 2), ("r", 0, 0, 1, 2), ("r",
    0, 0, 3, 2), ("r", 1, 0, 3, 2), ("sc", 1), ("r", 0, 1, 1, 1), ("r", 0, 1, 3, 1), ("hg", 1, 3), ("hg", 1, 0),
    ("r", 0, 1, 0, 1), ("hg", 1, 1), ("hg", 1, 2), ("hg", 2, 0), ("r", 0, 0, 0, 2), ("r", 1, 0, 2, 3), ("hg", 2, 3),
    ("r", 1, 0, 1, 2), ("r", 0, 2, 2, 1), ("hg", 2, 2), ("hg", 2, 1), ("r", 0, 2, 3, 1), ("r", 1, 0, 0, 2), ("r", 0,
    2, 1, 1), ("r", 0, 1, 2, 1), ("r", 0, 2, 0, 1), ("r", 0, 0, 1, 3), ("r", 1, 0, 3, 3), ("r", 0, 0, 3, 3), ("r",
    0, 0, 2, 3), ("r", 0, 1, 1, 2), ("r", 1, 1, 3, 1), ("r", 0, 1, 3, 2), ("r", 1, 1, 1, 1), ("r", 1, 1, 0, 1),
    ("r", 0, 1, 0, 2), ("r", 1, 1, 2, 1), ("r", 0, 2, 2, 2), ("r", 1, 2, 3, 1), ("r", 1, 2, 2, 1), ("r", 1, 2, 0,
    1), ("r", 1, 0, 1, 3), ("r", 0, 0, 0, 3), ("r", 1, 2, 1, 1), ("r", 0, 2, 3, 2), ("r", 0, 2, 0, 2), ("r", 1, 0,
    0, 3), ("r", 0, 2, 1, 2), ("r", 0, 1, 2, 2), ("mh", 0, 1), ("r", 0, 1, 3, 3), ("r", 0, 1, 1, 3), ("r", 1, 1, 1,
    2), ("r", 1, 1, 3, 2), ("r", 1, 1, 2, 2), ("r", 1, 1, 0, 2), ("r", 0, 2, 2, 3), ("r", 0, 1, 0, 3), ("r", 1, 2,
    2, 2), ("r", 1, 2, 3, 2), ("r", 1, 2, 0, 2), ("r", 1, 2, 1, 2), ("md", 0, 1), ("r", 0, 2, 3, 3), ("mh", 0, 0),
    ("md", 0, 0), ("r", 1, 1, 1, 3), ("r", 0, 1, 2, 3), ("r", 0, 2, 0, 3), ("r", 0, 0, 1, 5), ("r", 0, 0, 3, 5),
    ("r", 0, 2, 1, 3), ("mh", 1, 1), ("r", 1, 1, 3, 3), ("r", 1, 1, 2, 3), ("r", 1, 1, 0, 3), ("r", 1, 2, 2, 3),
    ("r", 1, 2, 3, 3), ("r", 1, 2, 0, 3), ("r", 1, 2, 1, 3), ("r", 1, 0, 3, 5), ("r", 0, 0, 2, 5), ("r", 0, 0, 0,
    5), ("r", 1, 0, 1, 5), ("r", 1, 0, 2, 5), ("r", 1, 0, 0, 5), ("mh", 1, 0), ("mh", 2, 0), ("r", 0, 1, 3, 5),
    ("r", 0, 0, 3, 6), ("mh", 2, 1), ("r", 0, 1, 1, 5), ("r", 0, 0, 1, 6), ("md", 1, 1), ("md", 1, 0), ("md", 2, 0),
    ("md", 2, 1), ("r", 0, 0, 2, 6), ("r", 0, 0, 0, 6), ("r", 1, 0, 3, 6), ("r", 1, 0, 1, 6), ("r", 0, 1, 2, 5),
    ("r", 1, 0, 2, 6), ("r", 0, 1, 0, 5), ("r", 0, 2, 2, 5), ("r", 1, 0, 0, 6), ("r", 0, 2, 0, 5), ("r", 0, 2, 3,
    5), ("r", 0, 1, 3, 6), ("r", 0, 0, 3, 7), ("r", 0, 1, 1, 6), ("r", 1, 1, 2, 5), ("r", 0, 2, 1, 5), ("r", 1, 1,
    0, 5), ("r", 0, 0, 1, 7), ("r", 1, 2, 2, 5), ("r", 1, 1, 1, 5), ("r", 1, 2, 0, 5), ("r", 1, 1, 3, 5), ("r", 1,
    2, 1, 5), ("r", 1, 2, 3, 5), ("r", 0, 0, 0, 7), ("r", 0, 0, 2, 7), ("r", 1, 0, 3, 7), ("r", 1, 0, 1, 7), ("r",
    0, 1, 2, 6), ("r", 1, 0, 0, 7), ("r", 1, 0, 2, 7), ("r", 0, 2, 2, 6), ("r", 0, 1, 0, 6), ("r", 0, 2, 3, 6),
    ("r", 0, 2, 0, 6), ("r", 0, 1, 3, 7), ("r", 0, 1, 1, 7), ("r", 1, 1, 2, 6), ("r", 0, 2, 1, 6), ("r", 1, 1, 0,
    6), ("r", 1, 2, 2, 6), ("r", 1, 1, 1, 6), ("r", 1, 1, 3, 6), ("r", 1, 2, 0, 6), ("r", 1, 2, 1, 6), ("r", 1, 2,
    3, 6), ("m3", 0), ("al", 0, 0), ("r", 0, 1, 2, 7), ("m5", 0), ("r", 0, 2, 3, 7), ("r", 0, 2, 2, 7), ("r", 0, 1,
    0, 7), ("r", 0, 2, 1, 7), ("en", 0, 0), ("r", 0, 2, 0, 7), ("al", 1, 0), ("r", 1, 1, 3, 7), ("r", 1, 1, 1, 7),
    ("r", 1, 1, 2, 7), ("r", 1, 2, 3, 7), ("r", 1, 2, 1, 7), ("r", 1, 1, 0, 7), ("en", 1, 0), ("r", 1, 2, 2, 7),
    ("m3", 1), ("r", 1, 2, 0, 7), ("m4", 3), ("m4", 2), ("al", 0, 1), ("m4", 0), ("m3", 2), ("m4", 1), ("al", 0, 2),
    ("m5", 1), ("al", 1, 1), ("en", 0, 1), ("m6", 2), ("m5", 2), ("m6", 3), ("m6", 0), ("al", 1, 2), ("en", 0, 2),
    ("m6", 1), ("en", 1, 1), ("en", 1, 2),
)


def place(turn, block):
    bits = [(block >> (3 - d)) & 1 for d in range(4)]
    index = 0
    for step in range(4):
        index = index * 2 + bits[(turn + step) % 4]
    return index


PLACES = [[place(j, k) for k in range(BLOCKS)] for j in range(4)]


def kernel(
    x_hbm, wg_hbm, wu_hbm, wd_hbm, ct_hbm,
    out, ig, gg, ug, dg,
    x_in, ct_in, xs, cts, wg, wu, wd,
    p_gu, r_gu, d_all, o_part, o_sib, o_z, o_sum,
    p_h0, p_h1, p_h2, p_h3, r_h0, r_h1, r_h2, r_h3, h0, h1, h2, h3,
    load_sem, ssem, rsem, zs_sem, zr_sem, ss_sem, sr_sem,
):
    p_hg, r_hg, h_all = (p_h0, p_h1, p_h2, p_h3), (r_h0, r_h1, r_h2, r_h3), (h0, h1, h2, h3)
    row, col = lax.axis_index("row"), lax.axis_index("col")
    y, x = row // 4, row % 4
    z, core = col // 2, col % 2
    partner = (
        (y * 4 + x + 1 - 2 * (x % 2), col),
        ((y + 1 - 2 * (y % 2)) * 4 + x, col),
        (y * 4 + 3 - x, col),
        ((3 - y) * 4 + x, col),
    )
    bits = (((x + 1) // 2) % 2, ((y + 1) // 2) % 2, x // 2, y // 2)
    mine = []
    for turn in range(4):
        index = 0
        for step in range(4):
            index = index * 2 + bits[(turn + step) % 4]
        mine.append(index)
    sibling = (row, z * 2 + 1 - core)
    along = {d: (row, lax.rem(z + d + CHIPS, CHIPS) * 2 + core) for d in SPOT if d != 0}

    loads = []
    for i, (src, dst) in enumerate(
        ((x_hbm, x_in), (ct_hbm, ct_in), (wg_hbm, wg), (wu_hbm, wu), (wd_hbm, wd))
    ):
        loads.append(pltpu.make_async_copy(src, dst, load_sem.at[i]))
        loads[-1].start()

    barrier = pltpu.get_barrier_semaphore()
    peers = list(along.values()) + list(partner) + [sibling]
    for peer in peers:
        pl.semaphore_signal(barrier, inc=1, device_id=peer, device_id_type=MESH)
    loads[0].wait()
    loads[1].wait()
    pl.semaphore_wait(barrier, len(peers))

    def remote(src, dst, send_sem, recv_sem, device):
        return pltpu.make_async_remote_copy(
            src_ref=src, dst_ref=dst, send_sem=send_sem, recv_sem=recv_sem,
            device_id=device, device_id_type=MESH,
        )

    stores, sources = (xs, cts), (x_in, ct_in)
    first_done = set()

    def once(key, act):
        if key not in first_done:
            first_done.add(key)
            act()

    def span(kind, who, group):
        lo, count = SPANS[group]
        return stores[kind].at[who, pl.ds(lo, count)]

    def shared(kind, who, group):
        lo, count = SPANS[group]
        return stores[kind].at[who, pl.ds(lo, count + (OWN if group == 0 else 0))]

    def gather_start(kind, group):
        buffer, own = stores[kind], sources[kind]
        for d in GROUPS[group]:
            back = d if d == 4 else -d
            remote(
                own, buffer.at[core, pl.ds(SPOT[back], OWN)],
                zs_sem.at[kind, group], zr_sem.at[kind, group], along[d],
            ).start()
        if group == 0:
            spot = buffer.at[core, pl.ds(SPOT[0], OWN)]
            remote(own, spot, ss_sem.at[kind, 0], sr_sem.at[kind, 0], sibling).start()
            spot[...] = own[...]

    def gather_share(kind, group):
        whole = span(kind, core, group)
        remote(whole, whole, zs_sem.at[kind, group], zr_sem.at[kind, group], sibling).wait_recv()
        remote(whole, whole, ss_sem.at[kind, group], sr_sem.at[kind, group], sibling).start()

    def gather_end(kind, group):
        def act():
            whole = shared(kind, 1 - core, group)
            remote(whole, whole, ss_sem.at[kind, group], sr_sem.at[kind, group], sibling).wait_recv()
        once(("gathered", kind, group), act)

    def gather_sent(kind, group):
        whole, both = span(kind, core, group), shared(kind, core, group)
        remote(whole, whole, zs_sem.at[kind, group], zr_sem.at[kind, group], sibling).wait_send()
        remote(both, both, ss_sem.at[kind, group], sr_sem.at[kind, group], sibling).wait_send()

    def rows_of(buffer, c):
        return buffer[:, FIRST[c]:FIRST[c] + HALF, :].reshape(2 * HALF, D)

    def turn_of(lane, j, step):
        return (j + 2) % 4 if lane == 1 and step < 4 else j

    def dim_of(lane, j, step):
        turn = turn_of(lane, j, step)
        return (turn + step) % 4 if step < 4 else (turn + 7 - step) % 4

    def ends(lane, c, j, step):
        own = mine[turn_of(lane, j, step)]
        if step < 4:
            part, arrive = (p_gu.at[c, j], r_gu.at[c, j]) if lane == 0 else (p_hg[j].at[c], r_hg[j].at[c])
            half = 8 >> step
            keep = own // half * half
            give = keep + half - 2 * half * (own // half % 2)
            return part.at[pl.ds(give, half)], arrive.at[pl.ds(BASE[step], half)]
        buffer = h_all[j].at[c] if lane == 0 else d_all.at[c, j]
        size = 1 << (step - 4)
        region = buffer.at[pl.ds(own // size * size, size)]
        return region, region

    SLOT = (0, 1, 2, 3, 2, 1, 0, 4)

    def copy_of(lane, c, j, step):
        turn = turn_of(lane, j, step)
        src, dst = ends(lane, c, j, step)
        return remote(
            src, dst, ssem.at[lane, c, turn, step % 2], rsem.at[lane, c, turn, SLOT[step]],
            partner[dim_of(lane, j, step)],
        )

    def launch(lane, c, j, step):
        if step >= 2:
            before = j
            if turn_of(lane, j, step) != turn_of(lane, j, step - 2):
                before = (j + 2) % 4
            copy_of(lane, c, before, step - 2).wait_send()
        copy_of(lane, c, j, step).start()

    def arrived(lane, c, j, step):
        if step < 4:
            copy_of(lane, c, j, step).wait_recv()
        else:
            own = mine[j]
            size = 1 << (step - 4)
            buffer = h_all[j].at[c] if lane == 0 else d_all.at[c, j]
            keep = own // size * size
            other = buffer.at[pl.ds(keep + size - 2 * size * (own // size % 2), size)]
            remote(
                other, other, ssem.at[lane, c, j, step % 2], rsem.at[lane, c, j, SLOT[step]],
                partner[dim_of(lane, j, step)],
            ).wait_recv()

    def reduce_step(lane, c, j, step):
        arrived(lane, c, j, step - 1)
        part, arrive = (p_gu.at[c, j], r_gu.at[c, j]) if lane == 0 else (p_hg[j].at[c], r_hg[j].at[c])
        index = mine[turn_of(lane, j, step)]
        half, wide = 8 >> step, 16 >> step
        start = index // wide * wide
        keep = index // half * half
        give = keep + half - 2 * half * (index // half % 2)

        def add(first):
            def body(i, carry):
                at = first + i
                part[at] = (
                    part[at].astype(jnp.float32) + arrive[BASE[step - 1] + at - start].astype(jnp.float32)
                ).astype(jnp.bfloat16)
                return carry

            lax.fori_loop(0, half, body, 0)

        add(give)
        launch(lane, c, j, step)
        add(keep)

    def total_of(lane, c, j):
        part, arrive = (p_gu.at[c, j], r_gu.at[c, j]) if lane == 0 else (p_hg[j].at[c], r_hg[j].at[c])
        return part[mine[turn_of(lane, j, 0)]].astype(jnp.float32) + arrive[BASE[3]].astype(jnp.float32)

    def store_partial(ref, turn, lo, value):
        width = value.shape[1]
        value = value.astype(jnp.bfloat16)
        for k in range(BLOCKS):
            ref[PLACES[turn][k], :, lo:lo + width] = value[k * ROWS:(k + 1) * ROWS, :]

    def ready(kind, c):
        for group in ((0,), (1,), (1, 2))[c]:
            gather_end(kind, group)

    def gate_up(c, j):
        once("w_gate", loads[2].wait)
        once("w_up", loads[3].wait)
        ready(0, c)
        value = rows_of(xs, c)
        lo, width = SETS[j]
        store_partial(p_gu.at[c, j], j, 0, jnp.dot(value, wg[:, lo:lo + width], preferred_element_type=jnp.float32))
        at = width
        lo, width = SETS[(j + 2) % 4]
        store_partial(p_gu.at[c, j], j, at, jnp.dot(value, wu[:, lo:lo + width], preferred_element_type=jnp.float32))
        launch(0, c, j, 0)

    def hidden_grad(c, j):
        once("w_down", loads[4].wait)
        ready(1, c)
        lo, width = SETS[j]
        value = lax.dot_general(rows_of(cts, c), wd[lo:lo + width, :], contract_cols, preferred_element_type=jnp.float32)
        store_partial(p_hg[j].at[c], (j + 2) % 4, 0, value)
        launch(1, c, j, 0)

    def make_hidden(c, pair):
        streams = (pair, pair + 2)
        for j in streams:
            arrived(0, c, j, 3)
        sums = {j: total_of(0, c, j) for j in streams}
        for j in streams:
            width = SETS[j][1]
            gate = sums[j][:, :width]
            up = sums[(j + 2) % 4][:, WIDE - width:]
            h_all[j][c, mine[j]] = (gate * jax.nn.sigmoid(gate) * up).astype(jnp.bfloat16)
            launch(0, c, j, 4)

    def make_deltas(c, pair):
        streams = (pair, pair + 2)
        for j in streams:
            arrived(1, c, j, 3)
        sums = {j: total_of(0, c, j) for j in streams}
        for j in streams:
            other = (j + 2) % 4
            width = SETS[j][1]
            gate = sums[j][:, :width]
            up = sums[other][:, WIDE - width:]
            grad = total_of(1, c, j)
            s = jax.nn.sigmoid(gate)
            d_all[c, j, mine[j], :, :width] = (grad * up * s * (1.0 + gate * (1.0 - s))).astype(jnp.bfloat16)
            d_all[c, other, mine[other], :, WIDE - width:] = (grad * gate * s).astype(jnp.bfloat16)
        for j in streams:
            launch(1, c, j, 4)

    def tokens(ref, c, j, lo, width):
        return jnp.concatenate([ref[c, PLACES[j][k], :, lo:lo + width] for k in range(BLOCKS)], axis=0)

    def hidden_of(c, j):
        return tokens(h_all[j], c, j, 0, SETS[j][1])

    def gate_delta_of(c, j):
        return tokens(d_all.at[:, j], c, j, 0, SETS[j][1])

    def up_delta_of(c, j):
        other = (j + 2) % 4
        return tokens(d_all.at[:, other], c, other, WIDE - SETS[j][1], SETS[j][1])

    def gathered(lane, c, j):
        once(("doubled", lane, c, j), lambda: arrived(lane, c, j, 7))

    def scatter_start(kind, c, total):
        o_part[kind, c] = total.astype(jnp.bfloat16).reshape(2, HALF, D)
        once(("sent", kind, c), lambda: gather_sent(kind, c))
        remote(
            o_part.at[kind, c, 1 - core], o_sib.at[kind, c], ss_sem.at[kind, c], sr_sem.at[2 + kind, c], sibling
        ).start()

    def scatter_along(kind, c):
        remote(
            o_part.at[kind, c, 1 - core], o_sib.at[kind, c], ss_sem.at[kind, c], sr_sem.at[2 + kind, c], sibling
        ).wait_recv()
        o_part[kind, c, core] = (
            o_part[kind, c, core].astype(jnp.float32) + o_sib[kind, c].astype(jnp.float32)
        ).astype(jnp.bfloat16)
        for d, lo, count, at in PARCELS[c]:
            back = d if d == 4 else -d
            remote(
                o_part.at[kind, c, core, pl.ds(lo, count)], o_z.at[kind, pl.ds(SPOT[back] + at, count)],
                zs_sem.at[kind, c], zr_sem.at[2 + kind, c], along[d],
            ).start()

    def landed(kind, c):
        lo, count = LANDED[c]
        whole = o_z.at[kind, pl.ds(lo, count)]
        return remote(whole, whole, zs_sem.at[kind, c], zr_sem.at[2 + kind, c], sibling)

    def scatter_end(kind, c):
        landed(kind, c).wait_recv()
        f32 = jnp.float32

        def own(lo, count):
            return o_part[kind, c, core, lo:lo + count, :].astype(f32)

        def come(d, at, count):
            return o_z[kind, SPOT[d] + at:SPOT[d] + at + count, :].astype(f32)

        if c == 0:
            o_sum[kind] = come(1, 0, OWN) + come(-1, 0, OWN)
            o_sum[kind, 0:32, :] += own(96, 32)
        elif c == 1:
            o_sum[kind] += come(3, 0, OWN) + come(-3, 0, OWN)
            o_sum[kind, 16:48, :] += come(4, 16, 32)
        else:
            o_sum[kind, 0:16, :] += come(4, 0, 16)
            o_sum[kind, 32:48, :] += own(0, 16)
            (out, ig)[kind][...] = (o_sum[kind] + come(2, 0, OWN) + come(-2, 0, OWN)).astype(jnp.bfloat16)

    def output_part(c):
        total = None
        for j in range(4):
            gathered(0, c, j)
            lo, width = SETS[j]
            term = jnp.dot(hidden_of(c, j), wd[lo:lo + width, :], preferred_element_type=jnp.float32)
            total = term if total is None else total + term
        scatter_start(0, c, total)

    def input_grad_part(c):
        for j in range(4):
            gathered(1, c, j)
        total = None
        for j in range(4):
            lo, width = SETS[j]
            term = lax.dot_general(
                gate_delta_of(c, j), wg[:, lo:lo + width], contract_cols, preferred_element_type=jnp.float32
            ) + lax.dot_general(
                up_delta_of(c, j), wu[:, lo:lo + width], contract_cols, preferred_element_type=jnp.float32
            )
            total = term if total is None else total + term
        scatter_start(1, c, total)

    def over_tokens(left, right):
        a = jnp.concatenate([left(c) for c in range(CHUNKS)], axis=0)
        b = jnp.concatenate([right(c) for c in range(CHUNKS)], axis=0)
        return lax.dot_general(a, b, contract_rows, preferred_element_type=jnp.float32).astype(jnp.bfloat16)

    def down_grad(j):
        for c in range(CHUNKS):
            gathered(0, c, j)
        lo, width = SETS[j]
        dg[lo:lo + width, :] = over_tokens(lambda c: hidden_of(c, j), lambda c: rows_of(cts, c))

    def input_side_grads(j):
        for c in range(CHUNKS):
            gathered(1, c, j)
            gathered(1, c, (j + 2) % 4)
        lo, width = SETS[j]
        for res, of in ((gg, gate_delta_of), (ug, up_delta_of)):
            res[:, lo:lo + width] = over_tokens(lambda c: rows_of(xs, c), lambda c: of(c, j))

    def halve_or_double(lane, c, j, step):
        if step < 4:
            reduce_step(lane, c, j, step)
        else:
            arrived(lane, c, j, step - 1)
            launch(lane, c, j, step)

    acts = {
        "x": lambda c: gather_start(0, c), "c": lambda c: gather_start(1, c),
        "sx": lambda c: gather_share(0, c), "sc": lambda c: gather_share(1, c),
        "gu": gate_up, "hg": hidden_grad, "r": halve_or_double, "mh": make_hidden, "md": make_deltas,
        "m3": output_part, "m5": input_grad_part, "al": scatter_along, "en": scatter_end,
        "m4": down_grad, "m6": input_side_grads,
    }
    for act, *where in ORDER:
        acts[act](*where)

    for lane in range(2):
        for c in range(CHUNKS):
            for j in range(4):
                for step in (6, 7):
                    copy_of(lane, c, j, step).wait_send()
    for kind in range(2):
        for c in range(CHUNKS):
            landed(kind, c).wait_send()
            remote(
                o_part.at[kind, c, 1 - core], o_sib.at[kind, c], ss_sem.at[kind, c], sr_sem.at[2 + kind, c], sibling
            ).wait_send()


def deliver(*refs):
    sources, results, sem = refs[:5], refs[5:10], refs[10]
    copies = []
    for src, dst in zip(sources, results):
        parts = 1 if src.shape[0] == OWN else PARTS
        step = src.shape[0] // parts
        for lo in range(0, src.shape[0], step):
            rows = pl.ds(lo, step)
            copies.append(pltpu.make_async_copy(src.at[rows], dst.at[rows], sem.at[len(copies)]))
    for copy in copies:
        copy.start()
    for copy in copies:
        copy.wait()


def local(inputs, w_gate, w_up, w_down, cotangent):
    bf16, f32 = jnp.bfloat16, jnp.float32
    vmem = pltpu.VMEM
    scratch = [
        vmem((OWN, D), bf16),
        vmem((OWN, D), bf16),
        vmem((2, CHUNKS * HALF, D), bf16),
        vmem((2, CHUNKS * HALF, D), bf16),
        vmem((D, F), bf16),
        vmem((D, F), bf16),
        vmem((F, D), bf16),
        vmem((CHUNKS, 4, BLOCKS, ROWS, WIDE), bf16),
        vmem((CHUNKS, 4, BLOCKS - 1, ROWS, WIDE), bf16),
        vmem((CHUNKS, 4, BLOCKS, ROWS, WIDE), bf16),
        vmem((2, CHUNKS, 2, HALF, D), bf16),
        vmem((2, CHUNKS, HALF, D), bf16),
        vmem((2, CHUNKS * HALF, D), bf16),
        vmem((2, OWN, D), f32),
    ]
    for count in (BLOCKS, BLOCKS - 1, BLOCKS):
        scratch += [vmem((CHUNKS, count, ROWS, width), bf16) for _, width in SETS]
    dma = pltpu.SemaphoreType.DMA
    scratch += [
        dma((5,)), dma((2, CHUNKS, 4, 2)), dma((2, CHUNKS, 4, 5)),
        dma((2, CHUNKS)), dma((4, CHUNKS)), dma((2, CHUNKS)), dma((4, CHUNKS)),
    ]
    whole = pl.BlockSpec(memory_space=pltpu.HBM)
    here = pl.BlockSpec(memory_space=pltpu.VMEM)
    results = (inputs, inputs, w_gate, w_up, w_down)
    held = pl.pallas_call(
        kernel,
        out_shape=tuple(pltpu.VMEM(a.shape, bf16) for a in results),
        in_specs=[whole] * 5,
        out_specs=[here] * 5,
        scratch_shapes=scratch,
        compiler_params=pltpu.CompilerParams(
            collective_id=0, has_side_effects=True, vmem_limit_bytes=40 * 2**20
        ),
    )(*[pltpu.with_memory_space_constraint(a, pltpu.HBM) for a in (inputs, w_gate, w_up, w_down, cotangent)])
    held = [pltpu.with_memory_space_constraint(a, pltpu.VMEM) for a in held]
    return pl.pallas_call(
        deliver,
        out_shape=tuple(jax.ShapeDtypeStruct(a.shape, bf16) for a in results),
        in_specs=[here] * 5,
        out_specs=[whole] * 5,
        scratch_shapes=[dma((2 + 3 * PARTS,))],
        compiler_params=pltpu.CompilerParams(vmem_limit_bytes=2**20),
    )(*held)


def solution(mesh):
    return jax.shard_map(
        local,
        mesh=mesh,
        in_specs=(P("col", "row"), P("row", "col"), P("row", "col"), P("col", "row"), P("col", "row")),
        out_specs=(P("col", "row"), P("col", "row"), P("row", "col"), P("row", "col"), P("col", "row")),
        check_vma=False,
    )
```

time: 491 us -> 118 us (0.24)
  waiting for transfers between devices: 380 us -> 0 us
  Pallas kernels: 0 us -> 117 us
  blocking collectives: 40.5 us -> 0 us
  matrix products: 37.9 us -> 0 us
  between operations: 14.2 us -> 0.8 us
  local copies, waits for them, and re-layouts: 9.35 us -> 0 us
  other arithmetic: 5.71 us -> 0 us
    reduce_scatter x4 -> x0, waiting for transfers between devices: 229 us -> none  [the longest x1 81.8 us: local(): lax.psum_scatter(lax.dot_general(row_block, w_down, contract_cols, prefer...]
    all_gather x3 -> x0, waiting for transfers between devices: 150 us -> none  [the longest x1 52.3 us: local(): lax.all_gather(gate_delta, 'row', axis=0, tiled=True)]
    pallas_call x0 -> x2, Pallas kernels: none -> 117 us  [the longest x1 115 us: local(): pl.pallas_call(kernel, out_shape=tuple((pltpu.VMEM(a.shape, bf16) for a i...]
    all_gather x2 -> x0, blocking collectives: 40.5 us -> none  [the longest x1 23.9 us: local(): inputs_all = lax.all_gather(inputs, 'col', axis=0, tiled=True)]
    dot_general x9 -> x0, matrix products: 37.9 us -> none  [the longest x1 5.31 us: local(): lax.dot_general(up_delta_all, w_up, contract_cols, preferred_element_type...]
    unnamed x10 -> x0, local copies, waits for them, and re-layouts: 9.35 us -> none
  transfers between devices with their start and end apart: 7 -> 0, of which waited for: 7 -> 0; matrix products, arithmetic and copies ran while one was open for 9% -> 0% of each run, Pallas kernels for 0% -> 0%
where the time goes in v2:
time: 118 us
  Pallas kernels  117 us (99%)
    pallas_call x1, Pallas kernels, local(): pl.pallas_call(kernel, out_shape=tuple((pltpu.VMEM(a.shape, bf16) for a i...  115 us
    pallas_call x1, Pallas kernels, local(): pl.pallas_call(deliver, out_shape=tuple((jax.ShapeDtypeStruct(a.shape, bf...  2.56 us

profile of v2, /device:TPU:1, one launch (start us, length us, event | category | flops | bytes accessed | tf_op | source)
XLA Modules:
  0.0 118.3 jit_solution(7790013846311736554)
XLA Ops:
  0.6 114.9 %shard_map.92 = (bf16[48,512]{1,0:T(8,128)(2,1)S(1)}, bf16[48,512]{1,0:T(8,128)(2,1)S(1)}, bf16[512,1792]{1,0:T(8,128)(2,1)S(1)}, bf16[512,1792]{1,0:T(8,128)(2,1)S(1)}, bf16[1792,512]{1,0:T(8,128)(2,1)S(1)}) custom-call(bf16[48,512]{1,0:T(8,128)(2,1)} %x_hbm.1, bf16[512,1792]{1,0:T(8,128)(2,1)} %wg_hbm.1, bf16[512,1792]{1,0:T(8,128)(2,1)} %wu_hbm.1, ...), custom_call_target="tpu_custom_call" | custom-call | tf_op jit(solution)/shard_map/pallas_call | solution.py:498
  115.6 2.6 %shard_map.93 = (bf16[48,512]{1,0:T(8,128)(2,1)}, bf16[48,512]{1,0:T(8,128)(2,1)}, bf16[512,1792]{1,0:T(8,128)(2,1)}, bf16[512,1792]{1,0:T(8,128)(2,1)}, bf16[1792,512]{1,0:T(8,128)(2,1)}) custom-call(bf16[48,512]{1,0:T(8,128)(2,1)S(1)} %get-tuple-element.10.refs_0_, bf16[48,512]{1,0:T(8,128)(2,1)S(1)} %get-tuple-element.11.refs_1_, ...), custom_call_target="tpu_custom_call" | custom-call | tf_op jit(solution)/shard_map/pallas_call | solution.py:509

commit v3 on v2

--- a/solution.py
+++ b/solution.py
@@ -18,55 +18,67 @@
 PARTS = 4
 BASE = (0, 8, 12, 14)
 
-SPOT = {1: 0, -1: 48, 0: 96, 2: 144, -2: 192, 4: 240, 3: 288, -3: 336}
+SPOT = {0: 0, 1: 48, -1: 96, 2: 144, -2: 192, 3: 240, 4: 288, -3: 336}
 FIRST = (0, 256, 128)
 GROUPS = ((1, -1), (4, 3, -3), (2, -2))
-SPANS = ((0, 96), (240, 144), (144, 96))
+SPANS = ((48, 96), (240, 144), (144, 96))
 PARCELS = (
-    ((1, 0, 48, 0), (-1, 48, 48, 0)),
-    ((4, 0, 32, 16), (3, 32, 48, 0), (-3, 80, 48, 0)),
-    ((4, 112, 16, 0), (2, 16, 48, 0), (-2, 64, 48, 0)),
+    ((1, 48, 48, 0), (-1, 96, 32, 0)),
+    ((4, 32, 48, 0), (3, 0, 32, 16), (-3, 80, 48, 0)),
+    ((3, 112, 16, 0), (2, 16, 48, 0), (-2, 64, 48, 0), (-1, 0, 16, 32)),
 )
-LANDED = ((0, 96), (256, 128), (144, 112))
+LANDED = (80, 128, 128)
 
 contract_rows = (((0,), (0,)), ((), ()))
 contract_cols = (((1,), (1,)), ((), ()))
 
 ORDER = (
-    ("x", 0), ("c", 0), ("sx", 0), ("x", 1), ("x", 2), ("sc", 0), ("c", 2), ("c", 1), ("gu", 0, 2), ("gu", 0, 3),
-    ("gu", 0, 1), ("hg", 0, 3), ("hg", 0, 0), ("hg", 0, 2), ("hg", 0, 1), ("gu", 0, 0), ("r", 1, 0, 2, 1), ("sx",
-    1), ("r", 0, 0, 2, 1), ("r", 0, 0, 3, 1), ("r", 0, 0, 1, 1), ("sx", 2), ("gu", 1, 3), ("gu", 1, 1), ("gu", 1,
-    0), ("gu", 2, 3), ("r", 1, 0, 3, 1), ("r", 1, 0, 1, 1), ("sc", 2), ("gu", 2, 2), ("r", 1, 0, 0, 1), ("r", 0, 0,
-    0, 1), ("r", 1, 0, 2, 2), ("gu", 2, 0), ("gu", 1, 2), ("gu", 2, 1), ("r", 0, 0, 2, 2), ("r", 0, 0, 1, 2), ("r",
-    0, 0, 3, 2), ("r", 1, 0, 3, 2), ("sc", 1), ("r", 0, 1, 1, 1), ("r", 0, 1, 3, 1), ("hg", 1, 3), ("hg", 1, 0),
-    ("r", 0, 1, 0, 1), ("hg", 1, 1), ("hg", 1, 2), ("hg", 2, 0), ("r", 0, 0, 0, 2), ("r", 1, 0, 2, 3), ("hg", 2, 3),
-    ("r", 1, 0, 1, 2), ("r", 0, 2, 2, 1), ("hg", 2, 2), ("hg", 2, 1), ("r", 0, 2, 3, 1), ("r", 1, 0, 0, 2), ("r", 0,
-    2, 1, 1), ("r", 0, 1, 2, 1), ("r", 0, 2, 0, 1), ("r", 0, 0, 1, 3), ("r", 1, 0, 3, 3), ("r", 0, 0, 3, 3), ("r",
-    0, 0, 2, 3), ("r", 0, 1, 1, 2), ("r", 1, 1, 3, 1), ("r", 0, 1, 3, 2), ("r", 1, 1, 1, 1), ("r", 1, 1, 0, 1),
-    ("r", 0, 1, 0, 2), ("r", 1, 1, 2, 1), ("r", 0, 2, 2, 2), ("r", 1, 2, 3, 1), ("r", 1, 2, 2, 1), ("r", 1, 2, 0,
-    1), ("r", 1, 0, 1, 3), ("r", 0, 0, 0, 3), ("r", 1, 2, 1, 1), ("r", 0, 2, 3, 2), ("r", 0, 2, 0, 2), ("r", 1, 0,
-    0, 3), ("r", 0, 2, 1, 2), ("r", 0, 1, 2, 2), ("mh", 0, 1), ("r", 0, 1, 3, 3), ("r", 0, 1, 1, 3), ("r", 1, 1, 1,
-    2), ("r", 1, 1, 3, 2), ("r", 1, 1, 2, 2), ("r", 1, 1, 0, 2), ("r", 0, 2, 2, 3), ("r", 0, 1, 0, 3), ("r", 1, 2,
-    2, 2), ("r", 1, 2, 3, 2), ("r", 1, 2, 0, 2), ("r", 1, 2, 1, 2), ("md", 0, 1), ("r", 0, 2, 3, 3), ("mh", 0, 0),
-    ("md", 0, 0), ("r", 1, 1, 1, 3), ("r", 0, 1, 2, 3), ("r", 0, 2, 0, 3), ("r", 0, 0, 1, 5), ("r", 0, 0, 3, 5),
-    ("r", 0, 2, 1, 3), ("mh", 1, 1), ("r", 1, 1, 3, 3), ("r", 1, 1, 2, 3), ("r", 1, 1, 0, 3), ("r", 1, 2, 2, 3),
-    ("r", 1, 2, 3, 3), ("r", 1, 2, 0, 3), ("r", 1, 2, 1, 3), ("r", 1, 0, 3, 5), ("r", 0, 0, 2, 5), ("r", 0, 0, 0,
-    5), ("r", 1, 0, 1, 5), ("r", 1, 0, 2, 5), ("r", 1, 0, 0, 5), ("mh", 1, 0), ("mh", 2, 0), ("r", 0, 1, 3, 5),
-    ("r", 0, 0, 3, 6), ("mh", 2, 1), ("r", 0, 1, 1, 5), ("r", 0, 0, 1, 6), ("md", 1, 1), ("md", 1, 0), ("md", 2, 0),
-    ("md", 2, 1), ("r", 0, 0, 2, 6), ("r", 0, 0, 0, 6), ("r", 1, 0, 3, 6), ("r", 1, 0, 1, 6), ("r", 0, 1, 2, 5),
-    ("r", 1, 0, 2, 6), ("r", 0, 1, 0, 5), ("r", 0, 2, 2, 5), ("r", 1, 0, 0, 6), ("r", 0, 2, 0, 5), ("r", 0, 2, 3,
-    5), ("r", 0, 1, 3, 6), ("r", 0, 0, 3, 7), ("r", 0, 1, 1, 6), ("r", 1, 1, 2, 5), ("r", 0, 2, 1, 5), ("r", 1, 1,
-    0, 5), ("r", 0, 0, 1, 7), ("r", 1, 2, 2, 5), ("r", 1, 1, 1, 5), ("r", 1, 2, 0, 5), ("r", 1, 1, 3, 5), ("r", 1,
-    2, 1, 5), ("r", 1, 2, 3, 5), ("r", 0, 0, 0, 7), ("r", 0, 0, 2, 7), ("r", 1, 0, 3, 7), ("r", 1, 0, 1, 7), ("r",
-    0, 1, 2, 6), ("r", 1, 0, 0, 7), ("r", 1, 0, 2, 7), ("r", 0, 2, 2, 6), ("r", 0, 1, 0, 6), ("r", 0, 2, 3, 6),
-    ("r", 0, 2, 0, 6), ("r", 0, 1, 3, 7), ("r", 0, 1, 1, 7), ("r", 1, 1, 2, 6), ("r", 0, 2, 1, 6), ("r", 1, 1, 0,
-    6), ("r", 1, 2, 2, 6), ("r", 1, 1, 1, 6), ("r", 1, 1, 3, 6), ("r", 1, 2, 0, 6), ("r", 1, 2, 1, 6), ("r", 1, 2,
-    3, 6), ("m3", 0), ("al", 0, 0), ("r", 0, 1, 2, 7), ("m5", 0), ("r", 0, 2, 3, 7), ("r", 0, 2, 2, 7), ("r", 0, 1,
-    0, 7), ("r", 0, 2, 1, 7), ("en", 0, 0), ("r", 0, 2, 0, 7), ("al", 1, 0), ("r", 1, 1, 3, 7), ("r", 1, 1, 1, 7),
-    ("r", 1, 1, 2, 7), ("r", 1, 2, 3, 7), ("r", 1, 2, 1, 7), ("r", 1, 1, 0, 7), ("en", 1, 0), ("r", 1, 2, 2, 7),
-    ("m3", 1), ("r", 1, 2, 0, 7), ("m4", 3), ("m4", 2), ("al", 0, 1), ("m4", 0), ("m3", 2), ("m4", 1), ("al", 0, 2),
-    ("m5", 1), ("al", 1, 1), ("en", 0, 1), ("m6", 2), ("m5", 2), ("m6", 3), ("m6", 0), ("al", 1, 2), ("en", 0, 2),
-    ("m6", 1), ("en", 1, 1), ("en", 1, 2),
+    ("c", 0), ("x", 0), ("sc", 0), ("c", 1), ("c", 2), ("hg", 0, 1), ("hg", 0, 2), ("sx", 0), ("hg", 0, 3), ("x",
+    2), ("hg", 0, 0), ("x", 1), ("gu", 0, 1), ("gu", 0, 2), ("gu", 0, 0), ("gu", 0, 3), ("r", 1, 0, 2, 1), ("k", 1,
+    0, 2, 1), ("r", 1, 0, 3, 1), ("r", 1, 0, 1, 1), ("k", 1, 0, 1, 1), ("k", 1, 0, 3, 1), ("r", 1, 0, 0, 1), ("k",
+    1, 0, 0, 1), ("sc", 1), ("hg", 1, 0), ("hg", 1, 1), ("sc", 2), ("hg", 1, 2), ("hg", 1, 3), ("r", 0, 0, 0, 1),
+    ("r", 0, 0, 1, 1), ("k", 0, 0, 1, 1), ("hg", 2, 2), ("r", 0, 0, 3, 1), ("k", 0, 0, 3, 1), ("k", 0, 0, 0, 1),
+    ("hg", 2, 0), ("sx", 2), ("r", 0, 0, 2, 1), ("r", 1, 0, 1, 2), ("k", 0, 0, 2, 1), ("r", 1, 0, 2, 2), ("k", 1, 0,
+    1, 2), ("hg", 2, 3), ("r", 1, 0, 0, 2), ("k", 1, 0, 0, 2), ("k", 1, 0, 2, 2), ("hg", 2, 1), ("r", 1, 0, 3, 2),
+    ("k", 1, 0, 3, 2), ("r", 1, 1, 2, 1), ("k", 1, 1, 2, 1), ("r", 1, 1, 0, 1), ("k", 1, 1, 0, 1), ("r", 1, 1, 3,
+    1), ("k", 1, 1, 3, 1), ("r", 1, 1, 1, 1), ("k", 1, 1, 1, 1), ("r", 1, 2, 2, 1), ("k", 1, 2, 2, 1), ("sx", 1),
+    ("r", 0, 0, 1, 2), ("k", 0, 0, 1, 2), ("r", 0, 0, 0, 2), ("r", 0, 0, 2, 2), ("k", 0, 0, 2, 2), ("k", 0, 0, 0,
+    2), ("gu", 1, 1), ("gu", 1, 3), ("gu", 1, 2), ("gu", 1, 0), ("r", 1, 0, 1, 3), ("r", 0, 0, 3, 2), ("k", 0, 0, 3,
+    2), ("gu", 2, 2), ("r", 1, 0, 0, 3), ("r", 1, 2, 3, 1), ("k", 1, 2, 3, 1), ("r", 1, 2, 0, 1), ("k", 1, 2, 0, 1),
+    ("k", 1, 0, 0, 3), ("r", 1, 2, 1, 1), ("k", 1, 2, 1, 1), ("gu", 2, 3), ("r", 1, 0, 2, 3), ("r", 1, 0, 3, 3),
+    ("k", 1, 0, 2, 3), ("k", 1, 0, 3, 3), ("k", 1, 0, 1, 3), ("gu", 2, 0), ("r", 1, 1, 1, 2), ("k", 1, 1, 1, 2),
+    ("gu", 2, 1), ("r", 1, 1, 3, 2), ("k", 1, 1, 3, 2), ("r", 1, 1, 2, 2), ("k", 1, 1, 2, 2), ("r", 1, 1, 0, 2),
+    ("k", 1, 1, 0, 2), ("r", 1, 2, 2, 2), ("k", 1, 2, 2, 2), ("r", 0, 0, 2, 3), ("k", 0, 0, 2, 3), ("r", 0, 0, 0,
+    3), ("k", 0, 0, 0, 3), ("r", 0, 0, 1, 3), ("k", 0, 0, 1, 3), ("r", 0, 1, 1, 1), ("k", 0, 1, 1, 1), ("r", 0, 1,
+    0, 1), ("k", 0, 1, 0, 1), ("r", 0, 1, 2, 1), ("k", 0, 1, 2, 1), ("r", 0, 1, 3, 1), ("k", 0, 1, 3, 1), ("r", 0,
+    0, 3, 3), ("k", 0, 0, 3, 3), ("r", 1, 2, 1, 2), ("k", 1, 2, 1, 2), ("r", 1, 1, 1, 3), ("k", 1, 1, 1, 3), ("r",
+    1, 2, 0, 2), ("k", 1, 2, 0, 2), ("r", 0, 2, 2, 1), ("k", 0, 2, 2, 1), ("r", 1, 2, 3, 2), ("k", 1, 2, 3, 2),
+    ("r", 0, 2, 0, 1), ("k", 0, 2, 0, 1), ("r", 0, 2, 1, 1), ("k", 0, 2, 1, 1), ("r", 0, 2, 3, 1), ("r", 1, 1, 2,
+    3), ("k", 0, 2, 3, 1), ("k", 1, 1, 2, 3), ("r", 1, 1, 0, 3), ("k", 1, 1, 0, 3), ("r", 1, 2, 2, 3), ("k", 1, 2,
+    2, 3), ("r", 1, 1, 3, 3), ("k", 1, 1, 3, 3), ("mh", 0, 0), ("md", 0, 0), ("r", 0, 1, 0, 2), ("k", 0, 1, 0, 2),
+    ("r", 0, 1, 1, 2), ("k", 0, 1, 1, 2), ("r", 0, 1, 3, 2), ("k", 0, 1, 3, 2), ("r", 1, 2, 1, 3), ("k", 1, 2, 1,
+    3), ("mh", 0, 1), ("r", 0, 1, 2, 2), ("md", 0, 1), ("k", 0, 1, 2, 2), ("r", 1, 2, 0, 3), ("k", 1, 2, 0, 3),
+    ("r", 0, 2, 0, 2), ("k", 0, 2, 0, 2), ("r", 0, 2, 2, 2), ("k", 0, 2, 2, 2), ("r", 0, 2, 1, 2), ("r", 0, 2, 3,
+    2), ("k", 0, 2, 1, 2), ("k", 0, 2, 3, 2), ("r", 0, 0, 2, 5), ("r", 1, 2, 3, 3), ("k", 1, 2, 3, 3), ("r", 0, 0,
+    1, 5), ("r", 1, 0, 2, 5), ("r", 0, 1, 0, 3), ("r", 0, 0, 0, 5), ("k", 0, 1, 0, 3), ("r", 0, 0, 3, 5), ("r", 1,
+    0, 0, 5), ("r", 0, 1, 2, 3), ("r", 0, 1, 3, 3), ("k", 0, 1, 3, 3), ("k", 0, 1, 2, 3), ("r", 1, 0, 3, 5), ("r",
+    1, 0, 1, 5), ("r", 0, 1, 1, 3), ("k", 0, 1, 1, 3), ("r", 0, 2, 0, 3), ("k", 0, 2, 0, 3), ("r", 0, 2, 2, 3),
+    ("k", 0, 2, 2, 3), ("r", 0, 2, 3, 3), ("k", 0, 2, 3, 3), ("r", 0, 2, 1, 3), ("k", 0, 2, 1, 3), ("r", 0, 0, 2,
+    6), ("r", 0, 0, 0, 6), ("r", 0, 0, 1, 6), ("r", 0, 0, 3, 6), ("mh", 1, 0), ("md", 1, 0), ("r", 1, 0, 0, 6),
+    ("r", 1, 0, 2, 6), ("mh", 1, 1), ("md", 1, 1), ("r", 1, 0, 1, 6), ("r", 1, 0, 3, 6), ("mh", 2, 0), ("md", 2, 0),
+    ("mh", 2, 1), ("md", 2, 1), ("r", 0, 0, 2, 7), ("r", 0, 0, 0, 7), ("r", 0, 0, 3, 7), ("r", 0, 0, 1, 7), ("r", 0,
+    1, 0, 5), ("r", 0, 1, 2, 5), ("r", 1, 1, 0, 5), ("r", 1, 1, 2, 5), ("r", 0, 1, 3, 5), ("r", 0, 1, 1, 5), ("r",
+    1, 1, 3, 5), ("r", 1, 1, 1, 5), ("r", 1, 0, 2, 7), ("r", 1, 0, 0, 7), ("r", 0, 2, 2, 5), ("r", 0, 2, 0, 5),
+    ("r", 1, 0, 1, 7), ("r", 1, 0, 3, 7), ("r", 1, 2, 2, 5), ("r", 1, 2, 0, 5), ("r", 0, 2, 3, 5), ("r", 0, 2, 1,
+    5), ("r", 1, 2, 3, 5), ("r", 1, 2, 1, 5), ("r", 0, 1, 1, 6), ("r", 0, 1, 3, 6), ("r", 0, 1, 0, 6), ("m3", 0),
+    ("r", 0, 1, 2, 6), ("r", 1, 1, 1, 6), ("r", 1, 1, 3, 6), ("r", 1, 1, 0, 6), ("al", 0, 0), ("r", 1, 1, 2, 6),
+    ("en", 0, 0), ("r", 0, 2, 1, 6), ("r", 0, 2, 3, 6), ("r", 0, 2, 0, 6), ("m5", 0), ("r", 1, 2, 0, 6), ("r", 1, 2,
+    3, 6), ("r", 0, 2, 2, 6), ("r", 1, 2, 1, 6), ("r", 0, 1, 2, 7), ("r", 1, 2, 2, 6), ("al", 1, 0), ("r", 0, 1, 0,
+    7), ("r", 0, 1, 1, 7), ("r", 0, 1, 3, 7), ("r", 1, 1, 2, 7), ("r", 1, 1, 0, 7), ("r", 1, 1, 1, 7), ("r", 1, 1,
+    3, 7), ("r", 0, 2, 2, 7), ("r", 0, 2, 0, 7), ("en", 1, 0), ("r", 0, 2, 3, 7), ("r", 0, 2, 1, 7), ("r", 1, 2, 2,
+    7), ("r", 1, 2, 0, 7), ("r", 1, 2, 3, 7), ("r", 1, 2, 1, 7), ("m3", 1), ("al", 0, 1), ("m5", 1), ("al", 1, 1),
+    ("m3", 2), ("m4", 0), ("m4", 3), ("al", 0, 2), ("m4", 1), ("m4", 2), ("en", 0, 1), ("m5", 2), ("m6", 2), ("al",
+    1, 2), ("m6", 3), ("m6", 1), ("en", 1, 1), ("m6", 0), ("en", 0, 2), ("en", 1, 2),
 )
 
 
@@ -87,7 +99,7 @@
     x_in, ct_in, xs, cts, wg, wu, wd,
     p_gu, r_gu, d_all, o_part, o_sib, o_z, o_sum,
     p_h0, p_h1, p_h2, p_h3, r_h0, r_h1, r_h2, r_h3, h0, h1, h2, h3,
-    load_sem, ssem, rsem, zs_sem, zr_sem, ss_sem, sr_sem,
+    load_sem, ssem, rsem, last_sem, zs_sem, zr_sem, ss_sem, sr_sem,
 ):
     p_hg, r_hg, h_all = (p_h0, p_h1, p_h2, p_h3), (r_h0, r_h1, r_h2, r_h3), (h0, h1, h2, h3)
     row, col = lax.axis_index("row"), lax.axis_index("col")
@@ -107,7 +119,7 @@
             index = index * 2 + bits[(turn + step) % 4]
         mine.append(index)
     sibling = (row, z * 2 + 1 - core)
-    along = {d: (row, lax.rem(z + d + CHIPS, CHIPS) * 2 + core) for d in SPOT if d != 0}
+    along = {d: (row, lax.rem(z + d * (1 - 2 * core) + CHIPS, CHIPS) * 2 + core) for d in SPOT if d != 0}
 
     loads = []
     for i, (src, dst) in enumerate(
@@ -144,7 +156,8 @@
 
     def shared(kind, who, group):
         lo, count = SPANS[group]
-        return stores[kind].at[who, pl.ds(lo, count + (OWN if group == 0 else 0))]
+        extra = OWN if group == 0 else 0
+        return stores[kind].at[who, pl.ds(lo - extra, count + extra)]
 
     def gather_start(kind, group):
         buffer, own = stores[kind], sources[kind]
@@ -198,22 +211,22 @@
         region = buffer.at[pl.ds(own // size * size, size)]
         return region, region
 
-    SLOT = (0, 1, 2, 3, 2, 1, 0, 4)
+    SLOT = (0, 1, 2, 3, 2, 1, 0)
+
+    def semaphores(lane, c, j, step):
+        if lane == 0:
+            leaving = ssem.at[0] if step < 4 else ssem.at[1 + j]
+        else:
+            leaving = ssem.at[5 + j] if step < 4 else ssem.at[9]
+        coming = last_sem.at[lane, c] if step == 7 else rsem.at[lane, c, turn_of(lane, j, step), SLOT[step]]
+        return leaving, coming
 
     def copy_of(lane, c, j, step):
-        turn = turn_of(lane, j, step)
-        src, dst = ends(lane, c, j, step)
         return remote(
-            src, dst, ssem.at[lane, c, turn, step % 2], rsem.at[lane, c, turn, SLOT[step]],
-            partner[dim_of(lane, j, step)],
+            *ends(lane, c, j, step), *semaphores(lane, c, j, step), partner[dim_of(lane, j, step)]
         )
 
     def launch(lane, c, j, step):
-        if step >= 2:
-            before = j
-            if turn_of(lane, j, step) != turn_of(lane, j, step - 2):
-                before = (j + 2) % 4
-            copy_of(lane, c, before, step - 2).wait_send()
         copy_of(lane, c, j, step).start()
 
     def arrived(lane, c, j, step):
@@ -226,12 +239,10 @@
             keep = own // size * size
             other = buffer.at[pl.ds(keep + size - 2 * size * (own // size % 2), size)]
             remote(
-                other, other, ssem.at[lane, c, j, step % 2], rsem.at[lane, c, j, SLOT[step]],
-                partner[dim_of(lane, j, step)],
+                other, other, *semaphores(lane, c, j, step), partner[dim_of(lane, j, step)]
             ).wait_recv()
 
-    def reduce_step(lane, c, j, step):
-        arrived(lane, c, j, step - 1)
+    def add_arrived(lane, c, j, step, given):
         part, arrive = (p_gu.at[c, j], r_gu.at[c, j]) if lane == 0 else (p_hg[j].at[c], r_hg[j].at[c])
         index = mine[turn_of(lane, j, step)]
         half, wide = 8 >> step, 16 >> step
@@ -239,19 +250,24 @@
         keep = index // half * half
         give = keep + half - 2 * half * (index // half % 2)
 
-        def add(first):
-            def body(i, carry):
-                at = first + i
-                part[at] = (
-                    part[at].astype(jnp.float32) + arrive[BASE[step - 1] + at - start].astype(jnp.float32)
-                ).astype(jnp.bfloat16)
-                return carry
-
-            lax.fori_loop(0, half, body, 0)
-
-        add(give)
+        first = give if given else keep
+
+        def body(i, carry):
+            at = first + i
+            part[at] = (
+                part[at].astype(jnp.float32) + arrive[BASE[step - 1] + at - start].astype(jnp.float32)
+            ).astype(jnp.bfloat16)
+            return carry
+
+        lax.fori_loop(0, half, body, 0)
+
+    def reduce_step(lane, c, j, step):
+        arrived(lane, c, j, step - 1)
+        add_arrived(lane, c, j, step, True)
         launch(lane, c, j, step)
-        add(keep)
+
+    def reduce_rest(lane, c, j, step):
+        add_arrived(lane, c, j, step, False)
 
     def total_of(lane, c, j):
         part, arrive = (p_gu.at[c, j], r_gu.at[c, j]) if lane == 0 else (p_hg[j].at[c], r_hg[j].at[c])
@@ -264,7 +280,7 @@
             ref[PLACES[turn][k], :, lo:lo + width] = value[k * ROWS:(k + 1) * ROWS, :]
 
     def ready(kind, c):
-        for group in ((0,), (1,), (1, 2))[c]:
+        for group in ((0,), (1,), (0, 1, 2))[c]:
             gather_end(kind, group)
 
     def gate_up(c, j):
@@ -316,24 +332,34 @@
         for j in streams:
             launch(1, c, j, 4)
 
-    def tokens(ref, c, j, lo, width):
-        return jnp.concatenate([ref[c, PLACES[j][k], :, lo:lo + width] for k in range(BLOCKS)], axis=0)
+    def tokens(ref, c, j, lo, width, half=None):
+        if half is None:
+            places = PLACES[j]
+        else:
+            places = [place + half * (8 >> (4 - j) % 4) for place in PLACES[j][:BLOCKS // 2]]
+        return jnp.concatenate([ref[c, place, :, lo:lo + width] for place in places], axis=0)
 
     def hidden_of(c, j):
         return tokens(h_all[j], c, j, 0, SETS[j][1])
 
-    def gate_delta_of(c, j):
-        return tokens(d_all.at[:, j], c, j, 0, SETS[j][1])
-
-    def up_delta_of(c, j):
+    def gate_delta_of(c, j, half=None):
+        return tokens(d_all.at[:, j], c, j, 0, SETS[j][1], half)
+
+    def up_delta_of(c, j, half=None):
         other = (j + 2) % 4
-        return tokens(d_all.at[:, other], c, other, WIDE - SETS[j][1], SETS[j][1])
-
-    def gathered(lane, c, j):
-        once(("doubled", lane, c, j), lambda: arrived(lane, c, j, 7))
+        return tokens(d_all.at[:, other], c, other, WIDE - SETS[j][1], SETS[j][1], half)
+
+    def gathered(lane, c):
+        def act():
+            size = p_gu.at[c, 0] if lane == 0 else d_all.at[c, :, pl.ds(0, 8)]
+            remote(size, size, ssem.at[1], last_sem.at[lane, c], sibling).wait_recv()
+        once(("doubled", lane, c), act)
 
     def scatter_start(kind, c, total):
         o_part[kind, c] = total.astype(jnp.bfloat16).reshape(2, HALF, D)
+        scatter_share(kind, c)
+
+    def scatter_share(kind, c):
         once(("sent", kind, c), lambda: gather_sent(kind, c))
         remote(
             o_part.at[kind, c, 1 - core], o_sib.at[kind, c], ss_sem.at[kind, c], sr_sem.at[2 + kind, c], sibling
@@ -354,8 +380,7 @@
             ).start()
 
     def landed(kind, c):
-        lo, count = LANDED[c]
-        whole = o_z.at[kind, pl.ds(lo, count)]
+        whole = o_z.at[kind, pl.ds(0, LANDED[c])]
         return remote(whole, whole, zs_sem.at[kind, c], zr_sem.at[2 + kind, c], sibling)
 
     def scatter_end(kind, c):
@@ -369,38 +394,46 @@
             return o_z[kind, SPOT[d] + at:SPOT[d] + at + count, :].astype(f32)
 
         if c == 0:
-            o_sum[kind] = come(1, 0, OWN) + come(-1, 0, OWN)
-            o_sum[kind, 0:32, :] += own(96, 32)
+            o_sum[kind] = own(0, OWN) + come(-1, 0, OWN)
+            o_sum[kind, 0:32, :] += come(1, 0, 32)
         elif c == 1:
-            o_sum[kind] += come(3, 0, OWN) + come(-3, 0, OWN)
-            o_sum[kind, 16:48, :] += come(4, 16, 32)
+            o_sum[kind] += come(3, 0, OWN) + come(4, 0, OWN)
+            o_sum[kind, 16:48, :] += come(-3, 16, 32)
         else:
-            o_sum[kind, 0:16, :] += come(4, 0, 16)
-            o_sum[kind, 32:48, :] += own(0, 16)
+            o_sum[kind, 0:16, :] += come(-3, 0, 16)
+            o_sum[kind, 32:48, :] += come(1, 32, 16)
             (out, ig)[kind][...] = (o_sum[kind] + come(2, 0, OWN) + come(-2, 0, OWN)).astype(jnp.bfloat16)
 
     def output_part(c):
+        gathered(0, c)
         total = None
         for j in range(4):
-            gathered(0, c, j)
             lo, width = SETS[j]
             term = jnp.dot(hidden_of(c, j), wd[lo:lo + width, :], preferred_element_type=jnp.float32)
             total = term if total is None else total + term
         scatter_start(0, c, total)
 
     def input_grad_part(c):
-        for j in range(4):
-            gathered(1, c, j)
-        total = None
-        for j in range(4):
-            lo, width = SETS[j]
-            term = lax.dot_general(
-                gate_delta_of(c, j), wg[:, lo:lo + width], contract_cols, preferred_element_type=jnp.float32
-            ) + lax.dot_general(
-                up_delta_of(c, j), wu[:, lo:lo + width], contract_cols, preferred_element_type=jnp.float32
-            )
-            total = term if total is None else total + term
-        scatter_start(1, c, total)
+        gathered(1, c)
+
+        def product(half):
+            total = None
+            for j in range(4):
+                lo, width = SETS[j]
+                term = lax.dot_general(
+                    gate_delta_of(c, j, half), wg[:, lo:lo + width], contract_cols, preferred_element_type=jnp.float32
+                ) + lax.dot_general(
+                    up_delta_of(c, j, half), wu[:, lo:lo + width], contract_cols, preferred_element_type=jnp.float32
+                )
+                total = term if total is None else total + term
+            return total
+
+        if c < CHUNKS - 1:
+            scatter_start(1, c, product(None))
+        else:
+            o_part[1, c, 1 - core] = product(1 - core).astype(jnp.bfloat16)
+            scatter_share(1, c)
+            o_part[1, c, core] = product(core).astype(jnp.bfloat16)
 
     def over_tokens(left, right):
         a = jnp.concatenate([left(c) for c in range(CHUNKS)], axis=0)
@@ -409,14 +442,13 @@
 
     def down_grad(j):
         for c in range(CHUNKS):
-            gathered(0, c, j)
+            gathered(0, c)
         lo, width = SETS[j]
         dg[lo:lo + width, :] = over_tokens(lambda c: hidden_of(c, j), lambda c: rows_of(cts, c))
 
     def input_side_grads(j):
         for c in range(CHUNKS):
-            gathered(1, c, j)
-            gathered(1, c, (j + 2) % 4)
+            gathered(1, c)
         lo, width = SETS[j]
         for res, of in ((gg, gate_delta_of), (ug, up_delta_of)):
             res[:, lo:lo + width] = over_tokens(lambda c: rows_of(xs, c), lambda c: of(c, j))
@@ -431,18 +463,19 @@
     acts = {
         "x": lambda c: gather_start(0, c), "c": lambda c: gather_start(1, c),
         "sx": lambda c: gather_share(0, c), "sc": lambda c: gather_share(1, c),
-        "gu": gate_up, "hg": hidden_grad, "r": halve_or_double, "mh": make_hidden, "md": make_deltas,
+        "gu": gate_up, "hg": hidden_grad, "r": halve_or_double, "k": reduce_rest, "mh": make_hidden, "md": make_deltas,
         "m3": output_part, "m5": input_grad_part, "al": scatter_along, "en": scatter_end,
         "m4": down_grad, "m6": input_side_grads,
     }
     for act, *where in ORDER:
         acts[act](*where)
 
-    for lane in range(2):
-        for c in range(CHUNKS):
-            for j in range(4):
-                for step in (6, 7):
-                    copy_of(lane, c, j, step).wait_send()
+    left = [(r_gu, 0)]
+    for j in range(4):
+        left += [(h_all[j].at[:, pl.ds(0, BLOCKS - 1)], 1 + j), (r_hg[j], 5 + j)]
+    left.append((d_all.at[:, :, pl.ds(0, BLOCKS - 1)], 9))
+    for size, i in left:
+        remote(size, size, ssem.at[i], last_sem.at[0, 0], sibling).wait_send()
     for kind in range(2):
         for c in range(CHUNKS):
             landed(kind, c).wait_send()
@@ -489,7 +522,7 @@
         scratch += [vmem((CHUNKS, count, ROWS, width), bf16) for _, width in SETS]
     dma = pltpu.SemaphoreType.DMA
     scratch += [
-        dma((5,)), dma((2, CHUNKS, 4, 2)), dma((2, CHUNKS, 4, 5)),
+        dma((5,)), dma((10,)), dma((2, CHUNKS, 4, 4)), dma((2, CHUNKS)),
         dma((2, CHUNKS)), dma((4, CHUNKS)), dma((2, CHUNKS)), dma((4, CHUNKS)),
     ]
     whole = pl.BlockSpec(memory_space=pltpu.HBM)

time: 118 us -> 115 us (0.975)
  Pallas kernels: 117 us -> 114 us
    pallas_call x1, Pallas kernels: 115 us -> 112 us  [local(): pl.pallas_call(kernel, out_shape=tuple((pltpu.VMEM(a.shape, bf16) for a i...]
where the time goes in v3:
time: 115 us
  Pallas kernels  114 us (99%)
    pallas_call x1, Pallas kernels, local(): pl.pallas_call(kernel, out_shape=tuple((pltpu.VMEM(a.shape, bf16) for a i...  112 us
    pallas_call x1, Pallas kernels, local(): pl.pallas_call(deliver, out_shape=tuple((jax.ShapeDtypeStruct(a.shape, bf...  2.56 us

profile of v3, /device:TPU:1, one launch (start us, length us, event | category | flops | bytes accessed | tf_op | source)
XLA Modules:
  0.0 115.1 jit_solution(15213811597457426588)
XLA Ops:
  0.6 111.7 %shard_map.92 = (bf16[48,512]{1,0:T(8,128)(2,1)S(1)}, bf16[48,512]{1,0:T(8,128)(2,1)S(1)}, bf16[512,1792]{1,0:T(8,128)(2,1)S(1)}, bf16[512,1792]{1,0:T(8,128)(2,1)S(1)}, bf16[1792,512]{1,0:T(8,128)(2,1)S(1)}) custom-call(bf16[48,512]{1,0:T(8,128)(2,1)} %x_hbm.1, bf16[512,1792]{1,0:T(8,128)(2,1)} %wg_hbm.1, bf16[512,1792]{1,0:T(8,128)(2,1)} %wu_hbm.1, ...), custom_call_target="tpu_custom_call" | custom-call | tf_op jit(solution)/shard_map/pallas_call | solution.py:531
  112.4 2.6 %shard_map.93 = (bf16[48,512]{1,0:T(8,128)(2,1)}, bf16[48,512]{1,0:T(8,128)(2,1)}, bf16[512,1792]{1,0:T(8,128)(2,1)}, bf16[512,1792]{1,0:T(8,128)(2,1)}, bf16[1792,512]{1,0:T(8,128)(2,1)}) custom-call(bf16[48,512]{1,0:T(8,128)(2,1)S(1)} %get-tuple-element.10.refs_0_, bf16[48,512]{1,0:T(8,128)(2,1)S(1)} %get-tuple-element.11.refs_1_, ...), custom_call_target="tpu_custom_call" | custom-call | tf_op jit(solution)/shard_map/pallas_call | solution.py:542

commit v4 on v3

v4 whole, which is shorter than its diff:
```python
import jax
import jax.numpy as jnp
from jax import lax
from jax.experimental import pallas as pl
from jax.experimental.pallas import tpu as pltpu
from jax.sharding import PartitionSpec as P

MESH = pl.DeviceIdType.MESH
ROWS = 16
OWN = 48
CHUNKS = 3
BLOCKS = 16
CHIPS = 8
SETS = ((0, 512), (512, 512), (1024, 384), (1408, 384))
D, F = 512, 1792
WIDE = 896
HALF = 128
PARTS = 4
BASE = (0, 8, 12, 14)

LAYOUT = (
    ((0, 0), (0, 1), (0, 2), (1, 0), (1, 1), (1, 2), (-1, 0), (-1, 1)),
    ((3, 1), (3, 2), (4, 0), (4, 1), (4, 2), (-3, 0), (-3, 1), (-3, 2)),
    ((3, 0), (2, 0), (2, 1), (-2, 0), (-2, 1), (2, 2), (-2, 2), (-1, 2)),
)
FAR = (1, -1, 2, -2, 3, 4, -3)
EARLY = 3
AHEAD = 5


def runs(c, first=0, count=8):
    found = []
    for i in range(first, first + count):
        d, part = LAYOUT[c][i]
        if found and found[-1][0] == d and found[-1][1] + found[-1][2] == part * ROWS:
            found[-1][2] += ROWS
        else:
            found.append([d, part * ROWS, ROWS, i * ROWS])
    return found


def back(d):
    return d if d == 4 else -d


contract_rows = (((0,), (0,)), ((), ()))
contract_cols = (((1,), (1,)), ((), ()))

ORDER = (
    ("c", 0), ("x", 0), ("ha", 3), ("ga", 0), ("ga", 1), ("ha", 0), ("ga", 3), ("ha", 2), ("ga", 2), ("ha", 1),
    ("sc", 0), ("c", 1), ("c", 2), ("hg", 0, 0), ("sx", 0), ("x", 1), ("hg", 0, 3), ("hg", 0, 1), ("hg", 0, 2),
    ("gu", 0, 1), ("gu", 0, 2), ("gu", 0, 0), ("gu", 0, 3), ("x", 2), ("r", 1, 0, 3, 1), ("k", 1, 0, 3, 1), ("r", 1,
    0, 0, 1), ("k", 1, 0, 0, 1), ("r", 1, 0, 2, 1), ("k", 1, 0, 2, 1), ("r", 1, 0, 1, 1), ("k", 1, 0, 1, 1), ("r",
    0, 0, 1, 1), ("k", 0, 0, 1, 1), ("r", 0, 0, 2, 1), ("sc", 1), ("k", 0, 0, 2, 1), ("r", 0, 0, 0, 1), ("k", 0, 0,
    0, 1), ("r", 0, 0, 3, 1), ("k", 0, 0, 3, 1), ("hg", 1, 1), ("r", 1, 0, 3, 2), ("r", 1, 0, 2, 2), ("k", 1, 0, 3,
    2), ("k", 1, 0, 2, 2), ("hg", 1, 2), ("hg", 1, 0), ("r", 1, 0, 0, 2), ("r", 1, 0, 1, 2), ("k", 1, 0, 0, 2),
    ("k", 1, 0, 1, 2), ("hg", 1, 3), ("sc", 2), ("hg", 2, 2), ("hg", 2, 3), ("hg", 2, 0), ("hg", 2, 1), ("r", 0, 0,
    1, 2), ("k", 0, 0, 1, 2), ("r", 0, 0, 2, 2), ("k", 0, 0, 2, 2), ("r", 1, 0, 2, 3), ("r", 0, 0, 0, 2), ("k", 0,
    0, 0, 2), ("k", 1, 0, 2, 3), ("r", 0, 0, 3, 2), ("k", 0, 0, 3, 2), ("r", 1, 0, 1, 3), ("k", 1, 0, 1, 3), ("sx",
    1), ("r", 1, 1, 2, 1), ("k", 1, 1, 2, 1), ("r", 1, 1, 1, 1), ("k", 1, 1, 1, 1), ("gu", 1, 0), ("r", 1, 0, 0, 3),
    ("r", 1, 0, 3, 3), ("k", 1, 0, 0, 3), ("k", 1, 0, 3, 3), ("gu", 1, 2), ("gu", 1, 3), ("sx", 2), ("gu", 1, 1),
    ("r", 1, 1, 0, 1), ("r", 1, 1, 3, 1), ("k", 1, 1, 0, 1), ("k", 1, 1, 3, 1), ("r", 1, 2, 3, 1), ("k", 1, 2, 3,
    1), ("gu", 2, 0), ("gu", 2, 3), ("gu", 2, 2), ("r", 0, 0, 3, 3), ("r", 0, 0, 2, 3), ("k", 0, 0, 2, 3), ("k", 0,
    0, 3, 3), ("gu", 2, 1), ("r", 0, 0, 0, 3), ("k", 0, 0, 0, 3), ("r", 1, 2, 2, 1), ("r", 1, 2, 0, 1), ("r", 0, 0,
    1, 3), ("k", 0, 0, 1, 3), ("r", 1, 2, 1, 1), ("k", 1, 2, 1, 1), ("k", 1, 2, 0, 1), ("k", 1, 2, 2, 1), ("r", 1,
    1, 2, 2), ("k", 1, 1, 2, 2), ("r", 1, 1, 1, 2), ("k", 1, 1, 1, 2), ("r", 0, 1, 2, 1), ("r", 0, 1, 3, 1), ("k",
    0, 1, 3, 1), ("k", 0, 1, 2, 1), ("r", 0, 1, 1, 1), ("k", 0, 1, 1, 1), ("r", 0, 1, 0, 1), ("k", 0, 1, 0, 1),
    ("r", 1, 1, 3, 2), ("k", 1, 1, 3, 2), ("r", 1, 1, 0, 2), ("k", 1, 1, 0, 2), ("r", 1, 2, 3, 2), ("k", 1, 2, 3,
    2), ("r", 0, 2, 0, 1), ("k", 0, 2, 0, 1), ("r", 0, 2, 1, 1), ("k", 0, 2, 1, 1), ("r", 0, 2, 3, 1), ("k", 0, 2,
    3, 1), ("r", 1, 2, 2, 2), ("mh", 0, 0), ("md", 0, 0), ("r", 0, 2, 2, 1), ("k", 0, 2, 2, 1), ("mh", 0, 1), ("md",
    0, 1), ("r", 1, 1, 2, 3), ("r", 1, 1, 1, 3), ("k", 1, 1, 2, 3), ("k", 1, 1, 1, 3), ("r", 1, 2, 1, 2), ("k", 1,
    2, 2, 2), ("k", 1, 2, 1, 2), ("r", 1, 2, 0, 2), ("k", 1, 2, 0, 2), ("r", 0, 1, 0, 2), ("k", 0, 1, 0, 2), ("r",
    0, 1, 3, 2), ("k", 0, 1, 3, 2), ("r", 0, 1, 1, 2), ("k", 0, 1, 1, 2), ("r", 0, 1, 2, 2), ("r", 1, 1, 0, 3),
    ("k", 0, 1, 2, 2), ("k", 1, 1, 0, 3), ("r", 1, 1, 3, 3), ("k", 1, 1, 3, 3), ("r", 1, 2, 3, 3), ("k", 1, 2, 3,
    3), ("r", 0, 0, 0, 5), ("r", 0, 2, 0, 2), ("k", 0, 2, 0, 2), ("r", 0, 0, 2, 5), ("r", 1, 0, 0, 5), ("r", 0, 2,
    1, 2), ("k", 0, 2, 1, 2), ("r", 0, 2, 3, 2), ("k", 0, 2, 3, 2), ("r", 1, 0, 2, 5), ("r", 1, 2, 2, 3), ("k", 1,
    2, 2, 3), ("r", 0, 0, 1, 5), ("r", 0, 0, 3, 5), ("r", 1, 2, 1, 3), ("k", 1, 2, 1, 3), ("r", 1, 0, 1, 5), ("r",
    1, 0, 3, 5), ("r", 1, 2, 0, 3), ("k", 1, 2, 0, 3), ("r", 0, 2, 2, 2), ("r", 0, 1, 3, 3), ("k", 0, 1, 3, 3),
    ("k", 0, 2, 2, 2), ("r", 0, 1, 0, 3), ("k", 0, 1, 0, 3), ("r", 0, 1, 2, 3), ("k", 0, 1, 2, 3), ("r", 0, 0, 0,
    6), ("r", 0, 1, 1, 3), ("k", 0, 1, 1, 3), ("r", 0, 0, 2, 6), ("r", 0, 2, 3, 3), ("k", 0, 2, 3, 3), ("r", 0, 2,
    0, 3), ("k", 0, 2, 0, 3), ("r", 0, 2, 1, 3), ("k", 0, 2, 1, 3), ("r", 0, 0, 3, 6), ("r", 1, 0, 2, 6), ("r", 0,
    0, 1, 6), ("r", 1, 0, 0, 6), ("r", 1, 0, 3, 6), ("r", 0, 2, 2, 3), ("k", 0, 2, 2, 3), ("r", 1, 0, 1, 6), ("mh",
    1, 1), ("md", 1, 1), ("mh", 1, 0), ("md", 1, 0), ("mh", 2, 1), ("r", 0, 0, 2, 7), ("r", 0, 0, 0, 7), ("md", 2,
    1), ("r", 0, 0, 3, 7), ("r", 0, 0, 1, 7), ("r", 1, 0, 0, 7), ("r", 1, 0, 2, 7), ("r", 1, 0, 3, 7), ("mh", 2, 0),
    ("r", 0, 1, 0, 5), ("r", 0, 1, 2, 5), ("r", 0, 1, 1, 5), ("md", 2, 0), ("r", 1, 0, 1, 7), ("r", 1, 1, 0, 5),
    ("r", 0, 1, 3, 5), ("r", 1, 1, 2, 5), ("r", 1, 1, 1, 5), ("r", 0, 2, 1, 5), ("r", 1, 1, 3, 5), ("r", 0, 2, 3,
    5), ("m3", 0), ("r", 0, 2, 2, 5), ("r", 1, 2, 2, 5), ("r", 1, 2, 1, 5), ("r", 1, 2, 3, 5), ("al", 0, 0), ("r",
    0, 2, 0, 5), ("r", 0, 1, 1, 6), ("r", 1, 2, 0, 5), ("m5", 0), ("r", 1, 1, 1, 6), ("r", 0, 1, 3, 6), ("r", 0, 1,
    0, 6), ("r", 0, 1, 2, 6), ("en", 0, 0), ("r", 1, 1, 0, 6), ("r", 1, 1, 2, 6), ("r", 0, 2, 1, 6), ("r", 1, 1, 3,
    6), ("r", 0, 2, 2, 6), ("al", 1, 0), ("r", 0, 2, 3, 6), ("r", 0, 2, 0, 6), ("r", 1, 2, 1, 6), ("r", 1, 2, 2, 6),
    ("r", 1, 2, 3, 6), ("r", 0, 1, 1, 7), ("r", 1, 2, 0, 6), ("r", 0, 1, 3, 7), ("r", 0, 1, 2, 7), ("r", 0, 1, 0,
    7), ("en", 1, 0), ("r", 1, 1, 1, 7), ("r", 1, 1, 3, 7), ("r", 1, 1, 2, 7), ("r", 1, 1, 0, 7), ("r", 0, 2, 1, 7),
    ("r", 0, 2, 3, 7), ("r", 0, 2, 2, 7), ("r", 0, 2, 0, 7), ("r", 1, 2, 1, 7), ("r", 1, 2, 3, 7), ("r", 1, 2, 2,
    7), ("m3", 1), ("r", 1, 2, 0, 7), ("al", 0, 1), ("m5", 1), ("al", 1, 1), ("m3", 2), ("m4", 1), ("m4", 0), ("al",
    0, 2), ("m4", 2), ("en", 0, 1), ("m4", 3), ("m5", 2), ("m5", 3), ("al", 1, 2), ("m6", 1), ("al", 1, 3), ("m6",
    2), ("m6", 3), ("m6", 0), ("en", 1, 1), ("en", 0, 2), ("en", 1, 2),
)


def place(turn, block):
    bits = [(block >> (3 - d)) & 1 for d in range(4)]
    index = 0
    for step in range(4):
        index = index * 2 + bits[(turn + step) % 4]
    return index


PLACES = [[place(j, i) for i in range(8)] for j in range(4)]


def at(turn, core, i):
    return PLACES[turn][i] if core == 0 else BLOCKS - 1 - PLACES[turn][i]


def kernel(
    x_hbm, wg_hbm, wu_hbm, wd_hbm, ct_hbm,
    out, ig, gg, ug, dg,
    x_in, ct_in, xs, cts, wg, wu, wd,
    p_gu, r_gu, d_all, o_part, o_sib, o_z, o_sum,
    p_h0, p_h1, p_h2, p_h3, r_h0, r_h1, r_h2, r_h3, h0, h1, h2, h3,
    load_sem, ssem, rsem, last_sem, zs_sem, zr_sem, ss_sem, sr_sem,
):
    p_hg, r_hg, h_all = (p_h0, p_h1, p_h2, p_h3), (r_h0, r_h1, r_h2, r_h3), (h0, h1, h2, h3)
    row, col = lax.axis_index("row"), lax.axis_index("col")
    y, x = row // 4, row % 4
    z, core = col // 2, col % 2
    partner = (
        (y * 4 + x + 1 - 2 * (x % 2), col),
        ((y + 1 - 2 * (y % 2)) * 4 + x, col),
        (y * 4 + 3 - x, col),
        ((3 - y) * 4 + x, col),
    )
    bits = (((x + 1) // 2) % 2, ((y + 1) // 2) % 2, x // 2, y // 2)
    mine = []
    for turn in range(4):
        index = 0
        for step in range(4):
            index = index * 2 + bits[(turn + step) % 4]
        mine.append(index)
    sibling = (row, z * 2 + 1 - core)
    along = {d: (row, lax.rem(z + d * (1 - 2 * core) + CHIPS, CHIPS) * 2 + core) for d in FAR}

    loads = []
    for i, (src, dst) in enumerate(
        ((x_hbm, x_in), (ct_hbm, ct_in), (wg_hbm, wg), (wu_hbm, wu), (wd_hbm, wd))
    ):
        loads.append(pltpu.make_async_copy(src, dst, load_sem.at[i]))
        loads[-1].start()

    barrier = pltpu.get_barrier_semaphore()
    peers = list(along.values()) + list(partner) + [sibling]
    for peer in peers:
        pl.semaphore_signal(barrier, inc=1, device_id=peer, device_id_type=MESH)
    loads[0].wait()
    loads[1].wait()
    pl.semaphore_wait(barrier, len(peers))

    def remote(src, dst, send_sem, recv_sem, device):
        return pltpu.make_async_remote_copy(
            src_ref=src, dst_ref=dst, send_sem=send_sem, recv_sem=recv_sem,
            device_id=device, device_id_type=MESH,
        )

    stores, sources = (xs, cts), (x_in, ct_in)
    first_done = set()

    def once(key, act):
        if key not in first_done:
            first_done.add(key)
            act()

    def region(kind, who, group):
        if group == 3:
            return stores[kind].at[who, pl.ds(0, OWN)]
        lo = OWN if group == 0 else group * HALF
        return stores[kind].at[who, pl.ds(lo, (group + 1) * HALF - lo)]

    def gather_start(kind, group):
        own = sources[kind]
        if group == 0:
            spot = region(kind, core, 3)
            remote(own, spot, ss_sem.at[kind, 3], sr_sem.at[kind, 3], sibling).start()
        for d, lo, count, first in runs(group):
            if d != 0:
                remote(
                    own.at[pl.ds(lo, count)], stores[kind].at[core, pl.ds(group * HALF + first, count)],
                    zs_sem.at[kind, group], zr_sem.at[kind, group], along[back(d)],
                ).start()
        if group == 0:
            spot[...] = own[...]

    def gather_share(kind, group):
        whole = region(kind, core, group)
        remote(whole, whole, zs_sem.at[kind, group], zr_sem.at[kind, group], sibling).wait_recv()
        remote(whole, whole, ss_sem.at[kind, group], sr_sem.at[kind, group], sibling).start()

    def gather_end(kind, group):
        def act():
            whole = region(kind, 1 - core, group)
            remote(whole, whole, ss_sem.at[kind, group], sr_sem.at[kind, group], sibling).wait_recv()
        once(("gathered", kind, group), act)

    def gather_sent(kind, group):
        whole = region(kind, core, group)
        if group < 3:
            remote(whole, whole, zs_sem.at[kind, group], zr_sem.at[kind, group], sibling).wait_send()
        remote(whole, whole, ss_sem.at[kind, group], sr_sem.at[kind, group], sibling).wait_send()

    def rows_of(buffer, c):
        return buffer[:, c * HALF:(c + 1) * HALF, :].reshape(2 * HALF, D)

    def turn_of(lane, j, step):
        return (j + 2) % 4 if lane == 1 and step < 4 else j

    def dim_of(lane, j, step):
        turn = turn_of(lane, j, step)
        return (turn + step) % 4 if step < 4 else (turn + 7 - step) % 4

    def ends(lane, c, j, step):
        own = mine[turn_of(lane, j, step)]
        if step < 4:
            part, arrive = (p_gu.at[c, j], r_gu.at[c, j]) if lane == 0 else (p_hg[j].at[c], r_hg[j].at[c])
            half = 8 >> step
            keep = own // half * half
            give = keep + half - 2 * half * (own // half % 2)
            return part.at[pl.ds(give, half)], arrive.at[pl.ds(BASE[step], half)]
        buffer = h_all[j].at[c] if lane == 0 else d_all.at[c, j]
        size = 1 << (step - 4)
        region = buffer.at[pl.ds(own // size * size, size)]
        return region, region

    SLOT = (0, 1, 2, 3, 2, 1, 0)

    def semaphores(lane, c, j, step):
        if lane == 0:
            leaving = ssem.at[0] if step < 4 else ssem.at[1 + j]
        else:
            leaving = ssem.at[5 + j] if step < 4 else ssem.at[9]
        coming = last_sem.at[lane * CHUNKS + c] if step == 7 else rsem.at[lane, c, turn_of(lane, j, step), SLOT[step]]
        return leaving, coming

    def copy_of(lane, c, j, step):
        return remote(
            *ends(lane, c, j, step), *semaphores(lane, c, j, step), partner[dim_of(lane, j, step)]
        )

    def launch(lane, c, j, step):
        if (lane, c, step) != (1, 2, 7):
            copy_of(lane, c, j, step).start()
            return
        high = mine[j] // 8
        for i in range(8):
            p = PLACES[j][i]
            block = d_all.at[c, j, pl.ds(p + (high if p < 8 else 1 - high) * (15 - 2 * p), 1)]
            leaving, coming = semaphores(lane, c, j, step)
            if i >= AHEAD:
                coming = last_sem.at[2 * CHUNKS]
            remote(block, block, leaving, coming, partner[dim_of(lane, j, step)]).start()

    def launch_blocks(lane, j, first, count):
        part, arrive = (p_gu.at[0, j], r_gu.at[0, j]) if lane == 0 else (p_hg[j].at[0], r_hg[j].at[0])
        turn = turn_of(lane, j, 0)
        high = mine[turn] // 8
        for i in range(first, first + count):
            p = PLACES[turn][i]
            q = p + (1 - high if p < 8 else high) * (15 - 2 * p)
            remote(
                part.at[pl.ds(q, 1)], arrive.at[pl.ds(q - 8 * (1 - high), 1)],
                *semaphores(lane, 0, j, 0), partner[dim_of(lane, j, 0)],
            ).start()

    def arrived(lane, c, j, step):
        if step < 4:
            copy_of(lane, c, j, step).wait_recv()
        else:
            own = mine[j]
            size = 1 << (step - 4)
            buffer = h_all[j].at[c] if lane == 0 else d_all.at[c, j]
            keep = own // size * size
            other = buffer.at[pl.ds(keep + size - 2 * size * (own // size % 2), size)]
            remote(
                other, other, *semaphores(lane, c, j, step), partner[dim_of(lane, j, step)]
            ).wait_recv()

    def add_arrived(lane, c, j, step, given):
        part, arrive = (p_gu.at[c, j], r_gu.at[c, j]) if lane == 0 else (p_hg[j].at[c], r_hg[j].at[c])
        index = mine[turn_of(lane, j, step)]
        half, wide = 8 >> step, 16 >> step
        start = index // wide * wide
        keep = index // half * half
        give = keep + half - 2 * half * (index // half % 2)

        first = give if given else keep

        def body(i, carry):
            where = first + i
            part[where] = (
                part[where].astype(jnp.float32) + arrive[BASE[step - 1] + where - start].astype(jnp.float32)
            ).astype(jnp.bfloat16)
            return carry

        lax.fori_loop(0, half, body, 0)

    def reduce_step(lane, c, j, step):
        arrived(lane, c, j, step - 1)
        add_arrived(lane, c, j, step, True)
        launch(lane, c, j, step)

    def reduce_rest(lane, c, j, step):
        add_arrived(lane, c, j, step, False)

    def total_of(lane, c, j):
        part, arrive = (p_gu.at[c, j], r_gu.at[c, j]) if lane == 0 else (p_hg[j].at[c], r_hg[j].at[c])
        return part[mine[turn_of(lane, j, 0)]].astype(jnp.float32) + arrive[BASE[3]].astype(jnp.float32)

    def store_partial(ref, turn, lo, value, first, count):
        width = value.shape[1]
        value = value.astype(jnp.bfloat16)
        for k in range(2 * count):
            ref[at(turn, k // count, first + k % count), :, lo:lo + width] = value[k * ROWS:(k + 1) * ROWS, :]

    def some_rows(buffer, c, first, count):
        lo = c * HALF + first * ROWS
        return buffer[:, lo:lo + count * ROWS, :].reshape(2 * count * ROWS, D)

    def gate_up_product(c, j, first, count):
        once("w_gate", loads[2].wait)
        once("w_up", loads[3].wait)
        value = some_rows(xs, c, first, count)
        ref, start = p_gu.at[c, j], 0
        for weight, (lo, width) in ((wg, SETS[j]), (wu, SETS[(j + 2) % 4])):
            term = jnp.dot(value, weight[:, lo:lo + width], preferred_element_type=jnp.float32)
            store_partial(ref, j, start, term, first, count)
            start += width

    def hidden_grad_product(c, j, first, count):
        once("w_down", loads[4].wait)
        lo, width = SETS[j]
        value = some_rows(cts, c, first, count)
        term = lax.dot_general(value, wd[lo:lo + width, :], contract_cols, preferred_element_type=jnp.float32)
        store_partial(p_hg[j].at[c], (j + 2) % 4, 0, term, first, count)

    def gate_up_early(j):
        gather_end(0, 3)
        gate_up_product(0, j, 0, EARLY)
        launch_blocks(0, j, 0, EARLY)

    def hidden_grad_early(j):
        gather_end(1, 3)
        hidden_grad_product(0, j, 0, EARLY)
        launch_blocks(1, j, 0, EARLY)

    def gate_up(c, j):
        gather_end(0, c)
        if c == 0:
            gate_up_product(0, j, EARLY, 8 - EARLY)
            launch_blocks(0, j, EARLY, 8 - EARLY)
        else:
            gate_up_product(c, j, 0, 8)
            launch(0, c, j, 0)

    def hidden_grad(c, j):
        gather_end(1, c)
        if c == 0:
            hidden_grad_product(0, j, EARLY, 8 - EARLY)
            launch_blocks(1, j, EARLY, 8 - EARLY)
        else:
            hidden_grad_product(c, j, 0, 8)
            launch(1, c, j, 0)

    def make_hidden(c, pair):
        streams = (pair, pair + 2)
        for j in streams:
            arrived(0, c, j, 3)
        sums = {j: total_of(0, c, j) for j in streams}
        for j in streams:
            width = SETS[j][1]
            gate = sums[j][:, :width]
            up = sums[(j + 2) % 4][:, WIDE - width:]
            h_all[j][c, mine[j]] = (gate * jax.nn.sigmoid(gate) * up).astype(jnp.bfloat16)
            launch(0, c, j, 4)

    def make_deltas(c, pair):
        streams = (pair, pair + 2)
        for j in streams:
            arrived(1, c, j, 3)
        sums = {j: total_of(0, c, j) for j in streams}
        for j in streams:
            other = (j + 2) % 4
            width = SETS[j][1]
            gate = sums[j][:, :width]
            up = sums[other][:, WIDE - width:]
            grad = total_of(1, c, j)
            s = jax.nn.sigmoid(gate)
            d_all[c, j, mine[j], :, :width] = (grad * up * s * (1.0 + gate * (1.0 - s))).astype(jnp.bfloat16)
            d_all[c, other, mine[other], :, WIDE - width:] = (grad * gate * s).astype(jnp.bfloat16)
        for j in streams:
            launch(1, c, j, 4)

    def tokens(ref, c, j, lo, width, first=0, count=8):
        blocks = [ref[c, at(j, k // count, first + k % count), :, lo:lo + width] for k in range(2 * count)]
        return jnp.concatenate(blocks, axis=0)

    def hidden_of(c, j):
        return tokens(h_all[j], c, j, 0, SETS[j][1])

    def gate_delta_of(c, j, *some):
        return tokens(d_all.at[:, j], c, j, 0, SETS[j][1], *some)

    def up_delta_of(c, j, *some):
        other = (j + 2) % 4
        return tokens(d_all.at[:, other], c, other, WIDE - SETS[j][1], SETS[j][1], *some)

    def gathered(lane, c, ahead=False):
        def act(size, sem):
            remote(size, size, ssem.at[1], last_sem.at[sem], sibling).wait_recv()

        split = (lane, c) == (1, 2)
        if lane == 0:
            size = p_gu.at[c, 0]
        else:
            size = d_all.at[c, :, pl.ds(0, AHEAD if split else 8)]
        once(("doubled", lane, c), lambda: act(size, lane * CHUNKS + c))
        if split and not ahead:
            once("rest", lambda: act(d_all.at[c, :, pl.ds(0, 8 - AHEAD)], 2 * CHUNKS))

    def share_of(kind, c, first, count):
        rows = pl.ds(first * ROWS, count * ROWS)
        slot = c if first == 0 else 3
        return remote(
            o_part.at[kind, c, 1 - core, rows], o_sib.at[kind, c, rows],
            ss_sem.at[kind, slot], sr_sem.at[2 + kind, slot], sibling,
        )

    def scatter_start(kind, c, total, first=0, count=8):
        rows = count * ROWS
        o_part[kind, c, :, first * ROWS:first * ROWS + rows, :] = total.astype(jnp.bfloat16).reshape(2, rows, D)
        once(("sent", kind, c, first), lambda: gather_sent(kind, c if first == 0 else 3))
        share_of(kind, c, first, count).start()

    def scatter_along(kind, c, first=0, count=8):
        share_of(kind, c, first, count).wait_recv()
        lo, hi = first * ROWS, (first + count) * ROWS
        o_part[kind, c, core, lo:hi, :] = (
            o_part[kind, c, core, lo:hi, :].astype(jnp.float32) + o_sib[kind, c, lo:hi, :].astype(jnp.float32)
        ).astype(jnp.bfloat16)
        for d, row, rows, start in runs(c, first, count):
            if d != 0:
                remote(
                    o_part.at[kind, c, core, pl.ds(start, rows)],
                    o_z.at[kind, pl.ds(FAR.index(back(d)) * OWN + row, rows)],
                    zs_sem.at[kind, c], zr_sem.at[2 + kind, c], along[d],
                ).start()

    def landed(kind, c):
        whole = o_z.at[kind, pl.ds(0, HALF - (OWN if c == 0 else 0))]
        return remote(whole, whole, zs_sem.at[kind, c], zr_sem.at[2 + kind, c], sibling)

    def scatter_end(kind, c):
        landed(kind, c).wait_recv()
        for d, row, rows, start in runs(c):
            if d == 0:
                o_sum[kind] = o_part[kind, c, core, 0:OWN, :].astype(jnp.float32)
            else:
                spot = FAR.index(back(d)) * OWN + row
                o_sum[kind, row:row + rows, :] += o_z[kind, spot:spot + rows, :].astype(jnp.float32)
        if c == CHUNKS - 1:
            (out, ig)[kind][...] = o_sum[kind].astype(jnp.bfloat16)

    def output_part(c):
        gathered(0, c)
        total = None
        for j in range(4):
            lo, width = SETS[j]
            term = jnp.dot(hidden_of(c, j), wd[lo:lo + width, :], preferred_element_type=jnp.float32)
            total = term if total is None else total + term
        scatter_start(0, c, total)

    def input_grad_part(c):
        split = c >= CHUNKS - 1
        some = (((0, AHEAD), (AHEAD, 8 - AHEAD))[c - 2]) if split else (0, 8)
        gathered(1, min(c, 2), c == 2)
        total = None
        for j in range(4):
            lo, width = SETS[j]
            term = lax.dot_general(
                gate_delta_of(min(c, 2), j, *some), wg[:, lo:lo + width], contract_cols,
                preferred_element_type=jnp.float32,
            ) + lax.dot_general(
                up_delta_of(min(c, 2), j, *some), wu[:, lo:lo + width], contract_cols,
                preferred_element_type=jnp.float32,
            )
            total = term if total is None else total + term
        scatter_start(1, min(c, 2), total, *some)

    def along_part(kind, c):
        if kind == 1 and c >= CHUNKS - 1:
            scatter_along(1, 2, *((0, AHEAD), (AHEAD, 8 - AHEAD))[c - 2])
        else:
            scatter_along(kind, c)

    def over_tokens(left, right):
        a = jnp.concatenate([left(c) for c in range(CHUNKS)], axis=0)
        b = jnp.concatenate([right(c) for c in range(CHUNKS)], axis=0)
        return lax.dot_general(a, b, contract_rows, preferred_element_type=jnp.float32).astype(jnp.bfloat16)

    def down_grad(j):
        for c in range(CHUNKS):
            gathered(0, c)
        lo, width = SETS[j]
        dg[lo:lo + width, :] = over_tokens(lambda c: hidden_of(c, j), lambda c: rows_of(cts, c))

    def input_side_grads(j):
        for c in range(CHUNKS):
            gathered(1, c)
        lo, width = SETS[j]
        for res, of in ((gg, gate_delta_of), (ug, up_delta_of)):
            res[:, lo:lo + width] = over_tokens(lambda c: rows_of(xs, c), lambda c: of(c, j))

    def halve_or_double(lane, c, j, step):
        if step < 4:
            reduce_step(lane, c, j, step)
        else:
            arrived(lane, c, j, step - 1)
            launch(lane, c, j, step)

    acts = {
        "x": lambda c: gather_start(0, c), "c": lambda c: gather_start(1, c),
        "sx": lambda c: gather_share(0, c), "sc": lambda c: gather_share(1, c),
        "gu": gate_up, "hg": hidden_grad, "r": halve_or_double, "k": reduce_rest, "mh": make_hidden, "md": make_deltas,
        "m3": output_part, "m5": input_grad_part, "al": along_part, "ga": gate_up_early, "ha": hidden_grad_early, "en": scatter_end,
        "m4": down_grad, "m6": input_side_grads,
    }
    for act, *where in ORDER:
        acts[act](*where)

    left = [(r_gu, 0)]
    for j in range(4):
        left += [(h_all[j].at[:, pl.ds(0, BLOCKS - 1)], 1 + j), (r_hg[j], 5 + j)]
    left.append((d_all.at[:, :, pl.ds(0, BLOCKS - 1)], 9))
    for size, i in left:
        remote(size, size, ssem.at[i], last_sem.at[0], sibling).wait_send()
    gather_sent(0, 3)
    for kind in range(2):
        for c in range(CHUNKS):
            landed(kind, c).wait_send()
            if (kind, c) == (1, 2):
                share_of(1, 2, 0, AHEAD).wait_send()
                share_of(1, 2, AHEAD, 8 - AHEAD).wait_send()
            else:
                share_of(kind, c, 0, 8).wait_send()


def deliver(*refs):
    sources, results, sem = refs[:5], refs[5:10], refs[10]
    copies = []
    for src, dst in zip(sources, results):
        parts = 1 if src.shape[0] == OWN else PARTS
        step = src.shape[0] // parts
        for lo in range(0, src.shape[0], step):
            rows = pl.ds(lo, step)
            copies.append(pltpu.make_async_copy(src.at[rows], dst.at[rows], sem.at[len(copies)]))
    for copy in copies:
        copy.start()
    for copy in copies:
        copy.wait()


def local(inputs, w_gate, w_up, w_down, cotangent):
    bf16, f32 = jnp.bfloat16, jnp.float32
    vmem = pltpu.VMEM
    scratch = [
        vmem((OWN, D), bf16),
        vmem((OWN, D), bf16),
        vmem((2, CHUNKS * HALF, D), bf16),
        vmem((2, CHUNKS * HALF, D), bf16),
        vmem((D, F), bf16),
        vmem((D, F), bf16),
        vmem((F, D), bf16),
        vmem((CHUNKS, 4, BLOCKS, ROWS, WIDE), bf16),
        vmem((CHUNKS, 4, BLOCKS - 1, ROWS, WIDE), bf16),
        vmem((CHUNKS, 4, BLOCKS, ROWS, WIDE), bf16),
        vmem((2, CHUNKS, 2, HALF, D), bf16),
        vmem((2, CHUNKS, HALF, D), bf16),
        vmem((2, len(FAR) * OWN, D), bf16),
        vmem((2, OWN, D), f32),
    ]
    for count in (BLOCKS, BLOCKS - 1, BLOCKS):
        scratch += [vmem((CHUNKS, count, ROWS, width), bf16) for _, width in SETS]
    dma = pltpu.SemaphoreType.DMA
    scratch += [
        dma((5,)), dma((10,)), dma((2, CHUNKS, 4, 4)), dma((2 * CHUNKS + 1,)),
        dma((2, CHUNKS)), dma((4, CHUNKS)), dma((2, 4)), dma((4, 4)),
    ]
    whole = pl.BlockSpec(memory_space=pltpu.HBM)
    here = pl.BlockSpec(memory_space=pltpu.VMEM)
    results = (inputs, inputs, w_gate, w_up, w_down)
    held = pl.pallas_call(
        kernel,
        out_shape=tuple(pltpu.VMEM(a.shape, bf16) for a in results),
        in_specs=[whole] * 5,
        out_specs=[here] * 5,
        scratch_shapes=scratch,
        compiler_params=pltpu.CompilerParams(
            collective_id=0, has_side_effects=True, vmem_limit_bytes=40 * 2**20
        ),
    )(*[pltpu.with_memory_space_constraint(a, pltpu.HBM) for a in (inputs, w_gate, w_up, w_down, cotangent)])
    held = [pltpu.with_memory_space_constraint(a, pltpu.VMEM) for a in held]
    return pl.pallas_call(
        deliver,
        out_shape=tuple(jax.ShapeDtypeStruct(a.shape, bf16) for a in results),
        in_specs=[here] * 5,
        out_specs=[whole] * 5,
        scratch_shapes=[dma((2 + 3 * PARTS,))],
        compiler_params=pltpu.CompilerParams(vmem_limit_bytes=2**20),
    )(*held)


def solution(mesh):
    return jax.shard_map(
        local,
        mesh=mesh,
        in_specs=(P("col", "row"), P("row", "col"), P("row", "col"), P("col", "row"), P("col", "row")),
        out_specs=(P("col", "row"), P("col", "row"), P("row", "col"), P("row", "col"), P("col", "row")),
        check_vma=False,
    )
```

time: 115 us -> 114 us (level)
  no operation moved by 1% of the time
where the time goes in v4:
time: 114 us
  Pallas kernels  113 us (99%)
    pallas_call x1, Pallas kernels, local(): pl.pallas_call(kernel, out_shape=tuple((pltpu.VMEM(a.shape, bf16) for a i...  111 us
    pallas_call x1, Pallas kernels, local(): pl.pallas_call(deliver, out_shape=tuple((jax.ShapeDtypeStruct(a.shape, bf...  2.56 us

profile of v4, /device:TPU:1, one launch (start us, length us, event | category | flops | bytes accessed | tf_op | source)
XLA Modules:
  0.0 114.2 jit_solution(930594749392151661)
XLA Ops:
  0.6 110.9 %shard_map.92 = (bf16[48,512]{1,0:T(8,128)(2,1)S(1)}, bf16[48,512]{1,0:T(8,128)(2,1)S(1)}, bf16[512,1792]{1,0:T(8,128)(2,1)S(1)}, bf16[512,1792]{1,0:T(8,128)(2,1)S(1)}, bf16[1792,512]{1,0:T(8,128)(2,1)S(1)}) custom-call(bf16[48,512]{1,0:T(8,128)(2,1)} %x_hbm.1, bf16[512,1792]{1,0:T(8,128)(2,1)} %wg_hbm.1, bf16[512,1792]{1,0:T(8,128)(2,1)} %wu_hbm.1, ...), custom_call_target="tpu_custom_call" | custom-call | tf_op jit(solution)/shard_map/pallas_call | solution.py:598
  111.5 2.6 %shard_map.93 = (bf16[48,512]{1,0:T(8,128)(2,1)}, bf16[48,512]{1,0:T(8,128)(2,1)}, bf16[512,1792]{1,0:T(8,128)(2,1)}, bf16[512,1792]{1,0:T(8,128)(2,1)}, bf16[1792,512]{1,0:T(8,128)(2,1)}) custom-call(bf16[48,512]{1,0:T(8,128)(2,1)S(1)} %get-tuple-element.10.refs_0_, bf16[48,512]{1,0:T(8,128)(2,1)S(1)} %get-tuple-element.11.refs_1_, ...), custom_call_target="tpu_custom_call" | custom-call | tf_op jit(solution)/shard_map/pallas_call | solution.py:609

commit v5 on v4

--- a/solution.py
+++ b/solution.py
@@ -47,53 +47,53 @@
 contract_cols = (((1,), (1,)), ((), ()))
 
 ORDER = (
-    ("c", 0), ("x", 0), ("ha", 3), ("ga", 0), ("ga", 1), ("ha", 0), ("ga", 3), ("ha", 2), ("ga", 2), ("ha", 1),
-    ("sc", 0), ("c", 1), ("c", 2), ("hg", 0, 0), ("sx", 0), ("x", 1), ("hg", 0, 3), ("hg", 0, 1), ("hg", 0, 2),
-    ("gu", 0, 1), ("gu", 0, 2), ("gu", 0, 0), ("gu", 0, 3), ("x", 2), ("r", 1, 0, 3, 1), ("k", 1, 0, 3, 1), ("r", 1,
-    0, 0, 1), ("k", 1, 0, 0, 1), ("r", 1, 0, 2, 1), ("k", 1, 0, 2, 1), ("r", 1, 0, 1, 1), ("k", 1, 0, 1, 1), ("r",
-    0, 0, 1, 1), ("k", 0, 0, 1, 1), ("r", 0, 0, 2, 1), ("sc", 1), ("k", 0, 0, 2, 1), ("r", 0, 0, 0, 1), ("k", 0, 0,
-    0, 1), ("r", 0, 0, 3, 1), ("k", 0, 0, 3, 1), ("hg", 1, 1), ("r", 1, 0, 3, 2), ("r", 1, 0, 2, 2), ("k", 1, 0, 3,
-    2), ("k", 1, 0, 2, 2), ("hg", 1, 2), ("hg", 1, 0), ("r", 1, 0, 0, 2), ("r", 1, 0, 1, 2), ("k", 1, 0, 0, 2),
-    ("k", 1, 0, 1, 2), ("hg", 1, 3), ("sc", 2), ("hg", 2, 2), ("hg", 2, 3), ("hg", 2, 0), ("hg", 2, 1), ("r", 0, 0,
-    1, 2), ("k", 0, 0, 1, 2), ("r", 0, 0, 2, 2), ("k", 0, 0, 2, 2), ("r", 1, 0, 2, 3), ("r", 0, 0, 0, 2), ("k", 0,
-    0, 0, 2), ("k", 1, 0, 2, 3), ("r", 0, 0, 3, 2), ("k", 0, 0, 3, 2), ("r", 1, 0, 1, 3), ("k", 1, 0, 1, 3), ("sx",
-    1), ("r", 1, 1, 2, 1), ("k", 1, 1, 2, 1), ("r", 1, 1, 1, 1), ("k", 1, 1, 1, 1), ("gu", 1, 0), ("r", 1, 0, 0, 3),
-    ("r", 1, 0, 3, 3), ("k", 1, 0, 0, 3), ("k", 1, 0, 3, 3), ("gu", 1, 2), ("gu", 1, 3), ("sx", 2), ("gu", 1, 1),
-    ("r", 1, 1, 0, 1), ("r", 1, 1, 3, 1), ("k", 1, 1, 0, 1), ("k", 1, 1, 3, 1), ("r", 1, 2, 3, 1), ("k", 1, 2, 3,
-    1), ("gu", 2, 0), ("gu", 2, 3), ("gu", 2, 2), ("r", 0, 0, 3, 3), ("r", 0, 0, 2, 3), ("k", 0, 0, 2, 3), ("k", 0,
-    0, 3, 3), ("gu", 2, 1), ("r", 0, 0, 0, 3), ("k", 0, 0, 0, 3), ("r", 1, 2, 2, 1), ("r", 1, 2, 0, 1), ("r", 0, 0,
-    1, 3), ("k", 0, 0, 1, 3), ("r", 1, 2, 1, 1), ("k", 1, 2, 1, 1), ("k", 1, 2, 0, 1), ("k", 1, 2, 2, 1), ("r", 1,
-    1, 2, 2), ("k", 1, 1, 2, 2), ("r", 1, 1, 1, 2), ("k", 1, 1, 1, 2), ("r", 0, 1, 2, 1), ("r", 0, 1, 3, 1), ("k",
-    0, 1, 3, 1), ("k", 0, 1, 2, 1), ("r", 0, 1, 1, 1), ("k", 0, 1, 1, 1), ("r", 0, 1, 0, 1), ("k", 0, 1, 0, 1),
-    ("r", 1, 1, 3, 2), ("k", 1, 1, 3, 2), ("r", 1, 1, 0, 2), ("k", 1, 1, 0, 2), ("r", 1, 2, 3, 2), ("k", 1, 2, 3,
-    2), ("r", 0, 2, 0, 1), ("k", 0, 2, 0, 1), ("r", 0, 2, 1, 1), ("k", 0, 2, 1, 1), ("r", 0, 2, 3, 1), ("k", 0, 2,
-    3, 1), ("r", 1, 2, 2, 2), ("mh", 0, 0), ("md", 0, 0), ("r", 0, 2, 2, 1), ("k", 0, 2, 2, 1), ("mh", 0, 1), ("md",
-    0, 1), ("r", 1, 1, 2, 3), ("r", 1, 1, 1, 3), ("k", 1, 1, 2, 3), ("k", 1, 1, 1, 3), ("r", 1, 2, 1, 2), ("k", 1,
-    2, 2, 2), ("k", 1, 2, 1, 2), ("r", 1, 2, 0, 2), ("k", 1, 2, 0, 2), ("r", 0, 1, 0, 2), ("k", 0, 1, 0, 2), ("r",
-    0, 1, 3, 2), ("k", 0, 1, 3, 2), ("r", 0, 1, 1, 2), ("k", 0, 1, 1, 2), ("r", 0, 1, 2, 2), ("r", 1, 1, 0, 3),
-    ("k", 0, 1, 2, 2), ("k", 1, 1, 0, 3), ("r", 1, 1, 3, 3), ("k", 1, 1, 3, 3), ("r", 1, 2, 3, 3), ("k", 1, 2, 3,
-    3), ("r", 0, 0, 0, 5), ("r", 0, 2, 0, 2), ("k", 0, 2, 0, 2), ("r", 0, 0, 2, 5), ("r", 1, 0, 0, 5), ("r", 0, 2,
-    1, 2), ("k", 0, 2, 1, 2), ("r", 0, 2, 3, 2), ("k", 0, 2, 3, 2), ("r", 1, 0, 2, 5), ("r", 1, 2, 2, 3), ("k", 1,
-    2, 2, 3), ("r", 0, 0, 1, 5), ("r", 0, 0, 3, 5), ("r", 1, 2, 1, 3), ("k", 1, 2, 1, 3), ("r", 1, 0, 1, 5), ("r",
-    1, 0, 3, 5), ("r", 1, 2, 0, 3), ("k", 1, 2, 0, 3), ("r", 0, 2, 2, 2), ("r", 0, 1, 3, 3), ("k", 0, 1, 3, 3),
-    ("k", 0, 2, 2, 2), ("r", 0, 1, 0, 3), ("k", 0, 1, 0, 3), ("r", 0, 1, 2, 3), ("k", 0, 1, 2, 3), ("r", 0, 0, 0,
-    6), ("r", 0, 1, 1, 3), ("k", 0, 1, 1, 3), ("r", 0, 0, 2, 6), ("r", 0, 2, 3, 3), ("k", 0, 2, 3, 3), ("r", 0, 2,
-    0, 3), ("k", 0, 2, 0, 3), ("r", 0, 2, 1, 3), ("k", 0, 2, 1, 3), ("r", 0, 0, 3, 6), ("r", 1, 0, 2, 6), ("r", 0,
-    0, 1, 6), ("r", 1, 0, 0, 6), ("r", 1, 0, 3, 6), ("r", 0, 2, 2, 3), ("k", 0, 2, 2, 3), ("r", 1, 0, 1, 6), ("mh",
-    1, 1), ("md", 1, 1), ("mh", 1, 0), ("md", 1, 0), ("mh", 2, 1), ("r", 0, 0, 2, 7), ("r", 0, 0, 0, 7), ("md", 2,
-    1), ("r", 0, 0, 3, 7), ("r", 0, 0, 1, 7), ("r", 1, 0, 0, 7), ("r", 1, 0, 2, 7), ("r", 1, 0, 3, 7), ("mh", 2, 0),
-    ("r", 0, 1, 0, 5), ("r", 0, 1, 2, 5), ("r", 0, 1, 1, 5), ("md", 2, 0), ("r", 1, 0, 1, 7), ("r", 1, 1, 0, 5),
-    ("r", 0, 1, 3, 5), ("r", 1, 1, 2, 5), ("r", 1, 1, 1, 5), ("r", 0, 2, 1, 5), ("r", 1, 1, 3, 5), ("r", 0, 2, 3,
-    5), ("m3", 0), ("r", 0, 2, 2, 5), ("r", 1, 2, 2, 5), ("r", 1, 2, 1, 5), ("r", 1, 2, 3, 5), ("al", 0, 0), ("r",
-    0, 2, 0, 5), ("r", 0, 1, 1, 6), ("r", 1, 2, 0, 5), ("m5", 0), ("r", 1, 1, 1, 6), ("r", 0, 1, 3, 6), ("r", 0, 1,
-    0, 6), ("r", 0, 1, 2, 6), ("en", 0, 0), ("r", 1, 1, 0, 6), ("r", 1, 1, 2, 6), ("r", 0, 2, 1, 6), ("r", 1, 1, 3,
-    6), ("r", 0, 2, 2, 6), ("al", 1, 0), ("r", 0, 2, 3, 6), ("r", 0, 2, 0, 6), ("r", 1, 2, 1, 6), ("r", 1, 2, 2, 6),
-    ("r", 1, 2, 3, 6), ("r", 0, 1, 1, 7), ("r", 1, 2, 0, 6), ("r", 0, 1, 3, 7), ("r", 0, 1, 2, 7), ("r", 0, 1, 0,
-    7), ("en", 1, 0), ("r", 1, 1, 1, 7), ("r", 1, 1, 3, 7), ("r", 1, 1, 2, 7), ("r", 1, 1, 0, 7), ("r", 0, 2, 1, 7),
-    ("r", 0, 2, 3, 7), ("r", 0, 2, 2, 7), ("r", 0, 2, 0, 7), ("r", 1, 2, 1, 7), ("r", 1, 2, 3, 7), ("r", 1, 2, 2,
-    7), ("m3", 1), ("r", 1, 2, 0, 7), ("al", 0, 1), ("m5", 1), ("al", 1, 1), ("m3", 2), ("m4", 1), ("m4", 0), ("al",
-    0, 2), ("m4", 2), ("en", 0, 1), ("m4", 3), ("m5", 2), ("m5", 3), ("al", 1, 2), ("m6", 1), ("al", 1, 3), ("m6",
-    2), ("m6", 3), ("m6", 0), ("en", 1, 1), ("en", 0, 2), ("en", 1, 2),
+    ("x", 0), ("c", 0), ("ga", 0), ("ha", 0), ("ha", 2), ("ha", 3), ("ga", 3), ("ha", 1), ("ga", 2), ("ga", 1),
+    ("sx", 0), ("x", 1), ("x", 2), ("sc", 0), ("c", 1), ("c", 2), ("gu", 0, 2), ("gu", 0, 3), ("gu", 0, 1), ("hg",
+    0, 3), ("hg", 0, 1), ("gu", 0, 0), ("hg", 0, 0), ("hg", 0, 2), ("r", 0, 0, 2, 1), ("k", 0, 0, 2, 1), ("r", 0, 0,
+    3, 1), ("k", 0, 0, 3, 1), ("r", 0, 0, 1, 1), ("k", 0, 0, 1, 1), ("sx", 1), ("r", 0, 0, 0, 1), ("k", 0, 0, 0, 1),
+    ("r", 1, 0, 0, 1), ("k", 1, 0, 0, 1), ("r", 1, 0, 3, 1), ("k", 1, 0, 3, 1), ("r", 1, 0, 1, 1), ("k", 1, 0, 1,
+    1), ("gu", 1, 0), ("r", 1, 0, 2, 1), ("k", 1, 0, 2, 1), ("gu", 1, 3), ("gu", 1, 2), ("gu", 1, 1), ("sx", 2),
+    ("gu", 2, 3), ("r", 0, 0, 2, 2), ("r", 0, 0, 3, 2), ("k", 0, 0, 3, 2), ("k", 0, 0, 2, 2), ("gu", 2, 2), ("r", 0,
+    0, 1, 2), ("k", 0, 0, 1, 2), ("gu", 2, 0), ("r", 1, 0, 0, 2), ("r", 0, 0, 0, 2), ("k", 1, 0, 0, 2), ("k", 0, 0,
+    0, 2), ("gu", 2, 1), ("r", 1, 0, 3, 2), ("r", 1, 0, 1, 2), ("k", 1, 0, 3, 2), ("k", 1, 0, 1, 2), ("r", 1, 0, 2,
+    2), ("k", 1, 0, 2, 2), ("sc", 1), ("hg", 1, 1), ("hg", 1, 0), ("hg", 1, 2), ("hg", 1, 3), ("sc", 2), ("r", 0, 1,
+    3, 1), ("k", 0, 1, 3, 1), ("r", 0, 1, 2, 1), ("k", 0, 1, 2, 1), ("r", 0, 1, 0, 1), ("k", 0, 1, 0, 1), ("hg", 2,
+    3), ("hg", 2, 1), ("r", 0, 1, 1, 1), ("k", 0, 1, 1, 1), ("hg", 2, 0), ("r", 0, 0, 2, 3), ("k", 0, 0, 2, 3),
+    ("hg", 2, 2), ("r", 0, 0, 3, 3), ("k", 0, 0, 3, 3), ("r", 0, 2, 3, 1), ("k", 0, 2, 3, 1), ("r", 0, 2, 2, 1),
+    ("k", 0, 2, 2, 1), ("r", 0, 0, 1, 3), ("k", 0, 0, 1, 3), ("r", 0, 0, 0, 3), ("k", 0, 0, 0, 3), ("r", 0, 2, 0,
+    1), ("k", 0, 2, 0, 1), ("r", 1, 0, 3, 3), ("k", 1, 0, 3, 3), ("r", 1, 0, 2, 3), ("k", 1, 0, 2, 3), ("r", 1, 0,
+    0, 3), ("k", 1, 0, 0, 3), ("r", 0, 2, 1, 1), ("k", 0, 2, 1, 1), ("r", 1, 0, 1, 3), ("k", 1, 0, 1, 3), ("r", 1,
+    1, 2, 1), ("k", 1, 1, 2, 1), ("r", 1, 1, 1, 1), ("k", 1, 1, 1, 1), ("r", 1, 1, 0, 1), ("k", 1, 1, 0, 1), ("r",
+    1, 1, 3, 1), ("k", 1, 1, 3, 1), ("r", 0, 1, 3, 2), ("k", 0, 1, 3, 2), ("r", 0, 1, 2, 2), ("k", 0, 1, 2, 2),
+    ("r", 0, 1, 1, 2), ("k", 0, 1, 1, 2), ("r", 0, 1, 0, 2), ("k", 0, 1, 0, 2), ("r", 1, 2, 2, 1), ("k", 1, 2, 2,
+    1), ("r", 1, 2, 3, 1), ("k", 1, 2, 3, 1), ("r", 1, 2, 1, 1), ("k", 1, 2, 1, 1), ("r", 1, 2, 0, 1), ("k", 1, 2,
+    0, 1), ("r", 0, 2, 3, 2), ("k", 0, 2, 3, 2), ("mh", 0, 1), ("r", 0, 2, 2, 2), ("k", 0, 2, 2, 2), ("r", 0, 2, 0,
+    2), ("k", 0, 2, 0, 2), ("mh", 0, 0), ("md", 0, 0), ("r", 0, 2, 1, 2), ("k", 0, 2, 1, 2), ("md", 0, 1), ("r", 1,
+    1, 1, 2), ("k", 1, 1, 1, 2), ("r", 1, 1, 2, 2), ("k", 1, 1, 2, 2), ("r", 1, 1, 0, 2), ("k", 1, 1, 0, 2), ("r",
+    1, 1, 3, 2), ("k", 1, 1, 3, 2), ("r", 0, 1, 2, 3), ("k", 0, 1, 2, 3), ("r", 0, 1, 3, 3), ("k", 0, 1, 3, 3),
+    ("r", 0, 1, 1, 3), ("k", 0, 1, 1, 3), ("r", 0, 1, 0, 3), ("k", 0, 1, 0, 3), ("r", 1, 2, 1, 2), ("k", 1, 2, 1,
+    2), ("r", 1, 2, 2, 2), ("k", 1, 2, 2, 2), ("r", 0, 0, 1, 5), ("r", 1, 2, 3, 2), ("k", 1, 2, 3, 2), ("r", 0, 0,
+    3, 5), ("r", 1, 2, 0, 2), ("k", 1, 2, 0, 2), ("r", 0, 0, 0, 5), ("r", 0, 2, 3, 3), ("k", 0, 2, 3, 3), ("r", 0,
+    2, 2, 3), ("k", 0, 2, 2, 3), ("r", 0, 0, 2, 5), ("r", 1, 0, 0, 5), ("r", 0, 2, 0, 3), ("k", 0, 2, 0, 3), ("r",
+    1, 0, 1, 5), ("r", 1, 0, 2, 5), ("r", 1, 0, 3, 5), ("r", 1, 1, 0, 3), ("k", 1, 1, 0, 3), ("r", 1, 1, 1, 3),
+    ("r", 0, 2, 1, 3), ("k", 1, 1, 1, 3), ("k", 0, 2, 1, 3), ("r", 1, 1, 2, 3), ("k", 1, 1, 2, 3), ("r", 1, 1, 3,
+    3), ("k", 1, 1, 3, 3), ("mh", 1, 1), ("mh", 1, 0), ("r", 1, 2, 2, 3), ("k", 1, 2, 2, 3), ("r", 1, 2, 1, 3),
+    ("k", 1, 2, 1, 3), ("r", 1, 2, 0, 3), ("k", 1, 2, 0, 3), ("r", 0, 0, 3, 6), ("r", 0, 0, 1, 6), ("r", 0, 0, 0,
+    6), ("r", 1, 2, 3, 3), ("r", 0, 0, 2, 6), ("k", 1, 2, 3, 3), ("mh", 2, 0), ("r", 1, 0, 2, 6), ("r", 1, 0, 0, 6),
+    ("r", 1, 0, 3, 6), ("r", 1, 0, 1, 6), ("mh", 2, 1), ("r", 0, 1, 3, 5), ("md", 1, 0), ("r", 0, 1, 2, 5), ("md",
+    1, 1), ("r", 0, 1, 0, 5), ("r", 0, 1, 1, 5), ("md", 2, 0), ("r", 0, 0, 3, 7), ("md", 2, 1), ("r", 0, 0, 1, 7),
+    ("r", 0, 0, 2, 7), ("r", 0, 0, 0, 7), ("r", 0, 2, 2, 5), ("r", 0, 2, 0, 5), ("r", 1, 0, 2, 7), ("r", 1, 0, 0,
+    7), ("r", 1, 0, 3, 7), ("r", 1, 0, 1, 7), ("r", 0, 2, 1, 5), ("r", 0, 1, 3, 6), ("r", 1, 1, 0, 5), ("r", 0, 2,
+    3, 5), ("r", 0, 1, 2, 6), ("r", 1, 1, 2, 5), ("r", 1, 1, 3, 5), ("r", 0, 1, 1, 6), ("r", 1, 1, 1, 5), ("r", 1,
+    2, 2, 5), ("r", 1, 2, 0, 5), ("r", 0, 1, 0, 6), ("r", 1, 2, 1, 5), ("r", 1, 2, 3, 5), ("m3", 0), ("r", 0, 2, 0,
+    6), ("r", 0, 2, 2, 6), ("al", 0, 0), ("r", 0, 2, 1, 6), ("r", 0, 2, 3, 6), ("m5", 0), ("r", 1, 1, 0, 6), ("r",
+    1, 1, 3, 6), ("r", 1, 1, 1, 6), ("r", 0, 1, 2, 7), ("r", 0, 1, 3, 7), ("en", 0, 0), ("r", 0, 1, 0, 7), ("r", 1,
+    1, 2, 6), ("r", 0, 1, 1, 7), ("r", 1, 2, 1, 6), ("al", 1, 0), ("r", 1, 2, 3, 6), ("r", 1, 2, 2, 6), ("r", 1, 2,
+    0, 6), ("r", 0, 2, 2, 7), ("r", 0, 2, 3, 7), ("r", 0, 2, 0, 7), ("r", 0, 2, 1, 7), ("en", 1, 0), ("r", 1, 1, 3,
+    7), ("r", 1, 1, 0, 7), ("r", 1, 1, 1, 7), ("r", 1, 1, 2, 7), ("m3", 1), ("r", 1, 2, 2, 7), ("r", 1, 2, 1, 7),
+    ("al", 0, 1), ("r", 1, 2, 3, 7), ("r", 1, 2, 0, 7), ("m4", 1), ("m3", 2), ("m4", 2), ("m4", 3), ("al", 0, 2),
+    ("m4", 0), ("m5", 1), ("en", 0, 1), ("al", 1, 1), ("m5", 2), ("en", 0, 2), ("m5", 3), ("al", 1, 2), ("m6", 0),
+    ("m6", 1), ("al", 1, 3), ("m6", 3), ("m6", 2), ("en", 1, 1), ("en", 1, 2),
 )
 
 

time: 114 us -> 113 us (level)
    pallas_call x1, Pallas kernels: 111 us -> 110 us  [local(): pl.pallas_call(kernel, out_shape=tuple((pltpu.VMEM(a.shape, bf16) for a i...]
where the time goes in v5:
time: 113 us
  Pallas kernels  112 us (99%)
    pallas_call x1, Pallas kernels, local(): pl.pallas_call(kernel, out_shape=tuple((pltpu.VMEM(a.shape, bf16) for a i...  110 us
    pallas_call x1, Pallas kernels, local(): pl.pallas_call(deliver, out_shape=tuple((jax.ShapeDtypeStruct(a.shape, bf...  2.56 us

profile of v5, /device:TPU:1, one launch (start us, length us, event | category | flops | bytes accessed | tf_op | source)
XLA Modules:
  0.0 113.1 jit_solution(9968322477574306030)
XLA Ops:
  0.6 109.7 %shard_map.92 = (bf16[48,512]{1,0:T(8,128)(2,1)S(1)}, bf16[48,512]{1,0:T(8,128)(2,1)S(1)}, bf16[512,1792]{1,0:T(8,128)(2,1)S(1)}, bf16[512,1792]{1,0:T(8,128)(2,1)S(1)}, bf16[1792,512]{1,0:T(8,128)(2,1)S(1)}) custom-call(bf16[48,512]{1,0:T(8,128)(2,1)} %x_hbm.1, bf16[512,1792]{1,0:T(8,128)(2,1)} %wg_hbm.1, bf16[512,1792]{1,0:T(8,128)(2,1)} %wu_hbm.1, ...), custom_call_target="tpu_custom_call" | custom-call | tf_op jit(solution)/shard_map/pallas_call | solution.py:598
  110.4 2.6 %shard_map.93 = (bf16[48,512]{1,0:T(8,128)(2,1)}, bf16[48,512]{1,0:T(8,128)(2,1)}, bf16[512,1792]{1,0:T(8,128)(2,1)}, bf16[512,1792]{1,0:T(8,128)(2,1)}, bf16[1792,512]{1,0:T(8,128)(2,1)}) custom-call(bf16[48,512]{1,0:T(8,128)(2,1)S(1)} %get-tuple-element.10.refs_0_, bf16[48,512]{1,0:T(8,128)(2,1)S(1)} %get-tuple-element.11.refs_1_, ...), custom_call_target="tpu_custom_call" | custom-call | tf_op jit(solution)/shard_map/pallas_call | solution.py:609

commit v6 on v5

--- a/solution.py
+++ b/solution.py
@@ -15,7 +15,7 @@
 D, F = 512, 1792
 WIDE = 896
 HALF = 128
-PARTS = 4
+PARTS = 1
 BASE = (0, 8, 12, 14)
 
 LAYOUT = (
@@ -118,7 +118,7 @@
     x_in, ct_in, xs, cts, wg, wu, wd,
     p_gu, r_gu, d_all, o_part, o_sib, o_z, o_sum,
     p_h0, p_h1, p_h2, p_h3, r_h0, r_h1, r_h2, r_h3, h0, h1, h2, h3,
-    load_sem, ssem, rsem, last_sem, zs_sem, zr_sem, ss_sem, sr_sem,
+    load_sem, ssem, rsem, pair_sem, last_sem, zs_sem, zr_sem, ss_sem, sr_sem,
 ):
     p_hg, r_hg, h_all = (p_h0, p_h1, p_h2, p_h3), (r_h0, r_h1, r_h2, r_h3), (h0, h1, h2, h3)
     row, col = lax.axis_index("row"), lax.axis_index("col")
@@ -140,6 +140,10 @@
     sibling = (row, z * 2 + 1 - core)
     along = {d: (row, lax.rem(z + d * (1 - 2 * core) + CHIPS, CHIPS) * 2 + core) for d in FAR}
 
+    barrier = pltpu.get_barrier_semaphore()
+    peers = [along[d] for d in (4, 3, -3, 2, -2, 1, -1)] + list(partner) + [sibling]
+    for peer in peers:
+        pl.semaphore_signal(barrier, inc=1, device_id=peer, device_id_type=MESH)
     loads = []
     for i, (src, dst) in enumerate(
         ((x_hbm, x_in), (ct_hbm, ct_in), (wg_hbm, wg), (wu_hbm, wu), (wd_hbm, wd))
@@ -147,10 +151,6 @@
         loads.append(pltpu.make_async_copy(src, dst, load_sem.at[i]))
         loads[-1].start()
 
-    barrier = pltpu.get_barrier_semaphore()
-    peers = list(along.values()) + list(partner) + [sibling]
-    for peer in peers:
-        pl.semaphore_signal(barrier, inc=1, device_id=peer, device_id_type=MESH)
     loads[0].wait()
     loads[1].wait()
     pl.semaphore_wait(barrier, len(peers))
@@ -229,14 +229,19 @@
         region = buffer.at[pl.ds(own // size * size, size)]
         return region, region
 
-    SLOT = (0, 1, 2, 3, 2, 1, 0)
+    SLOT = (0, 1, 2, None, 2, 1, 0)
 
     def semaphores(lane, c, j, step):
         if lane == 0:
             leaving = ssem.at[0] if step < 4 else ssem.at[1 + j]
         else:
             leaving = ssem.at[5 + j] if step < 4 else ssem.at[9]
-        coming = last_sem.at[lane * CHUNKS + c] if step == 7 else rsem.at[lane, c, turn_of(lane, j, step), SLOT[step]]
+        if step == 7:
+            coming = last_sem.at[lane * CHUNKS + c]
+        elif step == 3:
+            coming = pair_sem.at[lane, c, j % 2]
+        else:
+            coming = rsem.at[lane, c, turn_of(lane, j, step), SLOT[step]]
         return leaving, coming
 
     def copy_of(lane, c, j, step):
@@ -368,10 +373,13 @@
             hidden_grad_product(c, j, 0, 8)
             launch(1, c, j, 0)
 
+    def pair_arrived(lane, c, pair):
+        size = r_gu.at[c, 0, pl.ds(0, 2 - lane)]
+        remote(size, size, ssem.at[0], pair_sem.at[lane, c, pair], sibling).wait_recv()
+
     def make_hidden(c, pair):
         streams = (pair, pair + 2)
-        for j in streams:
-            arrived(0, c, j, 3)
+        pair_arrived(0, c, pair)
         sums = {j: total_of(0, c, j) for j in streams}
         for j in streams:
             width = SETS[j][1]
@@ -382,8 +390,7 @@
 
     def make_deltas(c, pair):
         streams = (pair, pair + 2)
-        for j in streams:
-            arrived(1, c, j, 3)
+        pair_arrived(1, c, pair)
         sums = {j: total_of(0, c, j) for j in streams}
         for j in streams:
             other = (j + 2) % 4
@@ -589,7 +596,7 @@
         scratch += [vmem((CHUNKS, count, ROWS, width), bf16) for _, width in SETS]
     dma = pltpu.SemaphoreType.DMA
     scratch += [
-        dma((5,)), dma((10,)), dma((2, CHUNKS, 4, 4)), dma((2 * CHUNKS + 1,)),
+        dma((5,)), dma((10,)), dma((2, CHUNKS, 4, 3)), dma((2, CHUNKS, 2)), dma((2 * CHUNKS + 1,)),
         dma((2, CHUNKS)), dma((4, CHUNKS)), dma((2, 4)), dma((4, 4)),
     ]
     whole = pl.BlockSpec(memory_space=pltpu.HBM)

time: 113 us -> 113 us (level)
  no operation moved by 1% of the time
where the time goes in v6:
time: 113 us
  Pallas kernels  112 us (99%)
    pallas_call x1, Pallas kernels, local(): pl.pallas_call(kernel, out_shape=tuple((pltpu.VMEM(a.shape, bf16) for a i...  109 us
    pallas_call x1, Pallas kernels, local(): pl.pallas_call(deliver, out_shape=tuple((jax.ShapeDtypeStruct(a.shape, bf...  2.51 us

profile of v6, /device:TPU:1, one launch (start us, length us, event | category | flops | bytes accessed | tf_op | source)
XLA Modules:
  0.0 112.7 jit_solution(13392549103286374925)
XLA Ops:
  0.6 109.4 %shard_map.92 = (bf16[48,512]{1,0:T(8,128)(2,1)S(1)}, bf16[48,512]{1,0:T(8,128)(2,1)S(1)}, bf16[512,1792]{1,0:T(8,128)(2,1)S(1)}, bf16[512,1792]{1,0:T(8,128)(2,1)S(1)}, bf16[1792,512]{1,0:T(8,128)(2,1)S(1)}) custom-call(bf16[48,512]{1,0:T(8,128)(2,1)} %x_hbm.1, bf16[512,1792]{1,0:T(8,128)(2,1)} %wg_hbm.1, bf16[512,1792]{1,0:T(8,128)(2,1)} %wu_hbm.1, ...), custom_call_target="tpu_custom_call" | custom-call | tf_op jit(solution)/shard_map/pallas_call | solution.py:605
  110.0 2.5 %shard_map.93 = (bf16[48,512]{1,0:T(8,128)(2,1)}, bf16[48,512]{1,0:T(8,128)(2,1)}, bf16[512,1792]{1,0:T(8,128)(2,1)}, bf16[512,1792]{1,0:T(8,128)(2,1)}, bf16[1792,512]{1,0:T(8,128)(2,1)}) custom-call(bf16[48,512]{1,0:T(8,128)(2,1)S(1)} %get-tuple-element.10.refs_0_, bf16[48,512]{1,0:T(8,128)(2,1)S(1)} %get-tuple-element.11.refs_1_, ...), custom_call_target="tpu_custom_call" | custom-call | tf_op jit(solution)/shard_map/pallas_call | solution.py:616
